TPU v7x, 128 devices: a whole 4x4x4 slice. The times are simulated.
128 devices in a mesh: attn: 16 (over z, x), expert: 8 (over y, core).
Axes of the slice: x: 4, y: 4, z: 4, core: 2. Of those that a mesh axis runs over, the one named last changes fastest.
Arguments:
- residual: bfloat16 [512, 6144], P('attn'), may hold values from -90 to 90
- queries: bfloat16 [512, 6144], P('attn', 'expert'), may hold values from -100 to 100
- new_keys: bfloat16 [512, 1024], P('attn', 'expert'), may hold values from -4 to 4
- new_values: bfloat16 [512, 1024], P('attn', 'expert'), may hold values from -4 to 4
- key_cache: bfloat16 [512, 8, 320, 128], P('attn', 'expert'), may hold values from -4 to 4
- value_cache: bfloat16 [512, 8, 320, 128], P('attn', 'expert'), may hold values from -4 to 4
- cache_lengths: int32 [512], P('attn'), may hold values from 1 to 320, 81920 in all
- out_weight: bfloat16 [6144, 6144], P('expert'), may hold values from -0.109375 to 0.109375
- norm_gain: float32 [6144], replicated, may hold values from 0.1 to 1.9
- gate_weight: bfloat16 [6144, 49152], P(None, ('attn', 'expert')), may hold values from -0.078125 to 0.078125
- up_weight: bfloat16 [6144, 49152], P(None, ('attn', 'expert')), may hold values from -0.078125 to 0.078125
- down_weight: bfloat16 [49152, 6144], P(('attn', 'expert')), may hold values from -0.21875 to 0.21875
- routes: int32 [512, 2], P('attn'), may hold values from 0 to 3, all different within a row; in each aligned block of 32 rows (0 to 31, 32 to 63, ...) at most 24 rows name the same one
- route_gates: float32 [512, 2], P('attn'), may hold values from 0.2 to 1
Outputs:
- layer_out: float32 [512, 6144], P('attn', 'expert')
Inputs may be any that keep to these rules, and one draw needn't show every extreme that they name: Positions from cache_lengths[b] on are not part of sequence b's cache; some sequence fills all 320 positions. `routes`: the two experts of a row differ. Among the 32 rows of one attn index no expert is named more than 24 times, a bound that some block reaches in the rows of some attn index.
All inputs are finite; a program needn't handle non-finite values. No bound on the sum of `cache_lengths` on one device may be relied on, other than what follows from the above.
Results may differ from a plain program's by a relative error of at most 0.003.
Values may be sent and summed in bfloat16 or wider, within the bound.
No kernel may reach another device: no remote copies, remote signals or barrier semaphores. Data moves between devices by JAX's collectives and lax.ppermute only.
A program may use at most 128 MiB of HBM per device.

v0:
```python
import math

import jax
import jax.numpy as jnp
from jax import lax
from jax.sharding import PartitionSpec as P

EXPERTS = 4
CAP = 24


epsilon = 1e-05


def attend(queries, new_keys, new_values, key_cache, value_cache, cache_lengths):
    row_count, kv_groups, cache_span, head_width = key_cache.shape
    heads_per = queries.shape[1] // (kv_groups * head_width)
    score_scale = 1.0 / math.sqrt(head_width)
    query_heads = queries.reshape(row_count, kv_groups, heads_per, head_width)
    scores = (
        jnp.einsum("bghd,bgld->bghl", query_heads, key_cache, preferred_element_type=jnp.float32)
        * score_scale
    )
    fresh_scores = (
        jnp.einsum(
            "bghd,bgd->bgh",
            query_heads,
            new_keys.reshape(row_count, kv_groups, head_width),
            preferred_element_type=jnp.float32,
        )
        * score_scale
    )
    visible = (jnp.arange(cache_span)[None, :] < cache_lengths[:, None])[:, None, None, :]
    scores = jnp.where(visible, scores, -jnp.inf)
    largest = jnp.maximum(jnp.max(scores, axis=3), fresh_scores)
    exp_scores = jnp.exp(scores - largest[..., None])
    exp_fresh = jnp.exp(fresh_scores - largest)
    denominator = jnp.sum(exp_scores, axis=3) + exp_fresh
    weights = (exp_scores / denominator[..., None]).astype(jnp.bfloat16)
    weights_new = (exp_fresh / denominator).astype(jnp.bfloat16)
    mixture = jnp.einsum(
        "bghl,bgld->bghd", weights, value_cache, preferred_element_type=jnp.float32
    )
    mixture = mixture + weights_new.astype(jnp.float32)[..., None] * new_values.reshape(
        row_count, kv_groups, 1, head_width
    ).astype(jnp.float32)
    return mixture.reshape(row_count, kv_groups * heads_per * head_width).astype(jnp.bfloat16)


def layer_block(
    residual,
    queries,
    new_keys,
    new_values,
    key_cache,
    value_cache,
    cache_lengths,
    routes,
    route_gates,
    out_weight,
    norm_gain,
    gate_weight,
    up_weight,
    down_weight,
):
    row_count = residual.shape[0]
    model_width = residual.shape[1]
    pool_size = lax.axis_size("attn")
    way_count = lax.axis_size("expert")
    column = lax.axis_index("expert")
    column_share = model_width // way_count
    expert_count = EXPERTS
    group_size = pool_size // expert_count
    capacity = min(CAP, row_count)
    slot_total = pool_size * capacity
    attended = attend(queries, new_keys, new_values, key_cache, value_cache, cache_lengths)
    partial_value = jnp.dot(attended, out_weight, preferred_element_type=jnp.float32)
    full_mid = residual.astype(jnp.float32) + lax.psum(partial_value, "expert")
    normed = (
        full_mid
        * lax.rsqrt(jnp.mean(full_mid * full_mid, axis=1, keepdims=True) + epsilon)
        * norm_gain
    ).astype(jnp.bfloat16)
    middle = lax.dynamic_slice_in_dim(full_mid, column * column_share, column_share, 1)
    flat_routes = routes.reshape(-1)
    one_hot = (flat_routes[:, None] == jnp.arange(expert_count)[None, :]).astype(jnp.int32)
    slot_rank = jnp.sum((jnp.cumsum(one_hot, axis=0) - one_hot) * one_hot, axis=1)
    slot_index = flat_routes * capacity + slot_rank
    slot_match = (slot_index[:, None] == jnp.arange(expert_count * capacity)[None, :]).reshape(
        row_count, 2, expert_count * capacity
    )
    chosen = jnp.any(slot_match, axis=1).astype(jnp.bfloat16)
    blend_table = jnp.sum(slot_match.astype(jnp.float32) * route_gates[:, :, None], axis=1)
    outgoing = jnp.einsum("ts,tc->sc", chosen, normed, preferred_element_type=jnp.float32).astype(
        jnp.bfloat16
    )
    outgoing = jnp.repeat(
        outgoing.reshape(expert_count, capacity, outgoing.shape[1]), group_size, axis=0
    )
    arrived = lax.all_to_all(outgoing, "attn", split_axis=0, concat_axis=0, tiled=True)
    slot_block = arrived.reshape(slot_total, model_width)
    gate_sum = jnp.dot(slot_block, gate_weight, preferred_element_type=jnp.float32)
    up_sum = jnp.dot(slot_block, up_weight, preferred_element_type=jnp.float32)
    hidden = (jax.nn.silu(gate_sum) * up_sum).astype(jnp.bfloat16)
    produced = jnp.dot(hidden, down_weight, preferred_element_type=jnp.float32)
    returned = lax.all_to_all(
        produced.reshape(pool_size, capacity, model_width),
        "attn",
        split_axis=0,
        concat_axis=0,
        tiled=True,
    )
    merged = jnp.sum(returned.reshape(expert_count, group_size, capacity, model_width), axis=1)
    token_rows = jnp.dot(
        blend_table,
        merged.reshape(expert_count * capacity, model_width),
        precision=lax.Precision.HIGHEST,
    )
    expert_mix = lax.psum_scatter(token_rows, "expert", scatter_dimension=1, tiled=True)
    return middle + expert_mix


def on_device(
    residual,
    queries,
    new_keys,
    new_values,
    key_cache,
    value_cache,
    cache_lengths,
    out_weight,
    norm_gain,
    gate_weight,
    up_weight,
    down_weight,
    routes,
    route_gates,
):
    token_args = (
        residual,
        queries,
        new_keys,
        new_values,
        key_cache,
        value_cache,
        cache_lengths,
        routes,
        route_gates,
    )
    weight_args = (out_weight, norm_gain, gate_weight, up_weight, down_weight)
    return layer_block(*token_args + weight_args)


def solution(mesh):
    in_specs = (
        P("attn", None),
        P("attn", "expert"),
        P("attn", "expert"),
        P("attn", "expert"),
        P("attn", "expert", None, None),
        P("attn", "expert", None, None),
        P("attn"),
        P("expert", None),
        P(),
        P(None, ("attn", "expert")),
        P(None, ("attn", "expert")),
        P(("attn", "expert"), None),
        P("attn", None),
        P("attn", None),
    )
    out_specs = P("attn", "expert")
    return jax.shard_map(
        on_device, mesh=mesh, in_specs=in_specs, out_specs=out_specs, check_vma=False
    )
```

profile of v0, /device:TPU:0, one launch (start us, length us, event | category | flops | bytes accessed | tf_op | source)
XLA Modules:
  0.0 360.1 jit_solution(9745502125985071586)
XLA Ops:
  6.5 0.0 copy-start
  6.5 0.0 all-reduce.2.cloned.1.call-start
  6.5 1.0 reshape.129
  7.6 0.7 iota_compare_fusion
  8.3 0.9 fusion.34
  9.2 0.0 copy-done
  9.2 1.0 fusion.39
  10.2 0.2 fusion.25
  10.4 0.7 convert_element_type.43
  11.1 2.3 fusion.15
  13.5 0.0 copy-start.3
  13.5 0.0 copy-start.2
  13.5 6.3 %fusion.29 = f32[32,6144]{1,0:T(8,128)} fusion(bf16[768,6144]{1,0:T(8,128)(2,1)} %param.21, bf16[4,8,6,128]{3,2,1,0:T(8,128)(2,1)S(1)} %bitcast.47), kind=kOutput, calls=%fused_computation.30 | convolution fusion | flops 301989888 | bytes 10272768 | tf_op jit(solution)/shard_map/dot_general | solution.py:77
  19.8 0.0 all-reduce.2.cloned.1.call-update
  19.8 0.0 copy-done.3
  19.8 0.1 copy.27
  19.9 0.1 eq.29
  20.0 0.1 fusion.33
  20.1 0.1 reduce_window_sum.11
  20.2 0.2 select_reduce_fusion.1
  20.4 0.1 reduce_sum.49
  20.5 0.1 copy.28
  20.6 0.1 fusion.32
  20.7 63.4 %all-reduce.2.cloned.1.call-done = f32[32,6144]{1,0:T(8,128)} async-done(((f32[32,6144]{1,0:T(8,128)}), f32[32,6144]{1,0:T(8,128)}) %all-reduce.2.cloned.1.call-update) | async-done | bytes 786448 | tf_op jit(solution)/shard_map/psum | solution.py:78
  84.1 1.4 multiply_reduce_fusion
  85.5 0.0 copy-done.2
  85.5 0.5 convolution_convert_fusion
  86.1 0.0 slice-start
  86.1 0.5 broadcast_in_dim.16
  86.6 0.0 slice-start.1
  86.6 61.8 %all_to_all.10 = bf16[16,24,6144]{2,1,0:T(8,128)(2,1)S(1)} all-to-all(bf16[16,24,6144]{2,1,0:T(8,128)(2,1)S(1)} %bitcast.42), channel_id=1, replica_groups=mesh['attn'=16,'expert'=8] {'attn'}, dimensions={0} | all-to-all | bytes 9437184 | tf_op jit(solution)/shard_map/all_to_all | solution.py:100
  148.5 0.0 copy-start.1
  148.5 2.2 copy-done.1
  150.7 0.0 slice-done
  150.7 0.0 slice-done.1
  150.7 3.4 fusion.40
  154.1 14.0 %fusion.5 = f32[384,6144]{1,0:T(8,128)} fusion(bf16[384,6144]{1,0:T(8,128)(2,1)} %param.25, bf16[384,6144]{1,0:T(8,128)(2,1)} %bitcast.44, bf16[6144,384]{1,0:T(8,128)(2,1)} %param.24, f32[384,384]{1,0:T(8,128)} %fusion.40), kind=kOutput, calls=%fused_computation.8 | convolution fusion | flops 3624763392 | bytes 24182784 | tf_op jit(solution)/shard_map/dot_general | solution.py:105
  168.1 0.0 copy-start.4
  168.1 4.9 %all-to-all-start.1 = ((f32[16,24,6144]{2,1,0:T(8,128)}), f32[16,24,6144]{2,1,0:T(8,128)}, u32[]{:S(2)}, u32[]{:S(2)}) async-start(f32[16,24,6144]{2,1,0:T(8,128)} %bitcast.41), calls=%async_computation.1 | async-start | bytes 18874368 | tf_op jit(solution)/shard_map/all_to_all | solution.py:106
  173.0 0.0 reduce-scatter.2.cloned.1.call-start
  173.1 0.0 copy-done.4
  173.1 0.1 select_reduce_fusion
  173.2 132.3 %all-to-all-done.1 = f32[16,24,6144]{2,1,0:T(8,128)} async-done(((f32[16,24,6144]{2,1,0:T(8,128)}), f32[16,24,6144]{2,1,0:T(8,128)}, u32[]{:S(2)}, u32[]{:S(2)}) %all-to-all-start.1) | async-done | bytes 9437216 | tf_op jit(solution)/shard_map/all_to_all | solution.py:106
  305.4 4.7 %bitcast_reduce_fusion = f32[4,24,6144]{2,1,0:T(8,128)S(1)} fusion(f32[16,24,6144]{2,1,0:T(8,128)} %all-to-all-done.1), kind=kLoop, calls=%fused_computation | loop fusion | flops 1769472 | bytes 11796480 | tf_op jit(solution)/shard_map/reduce_sum | solution.py:113
  310.1 2.1 fusion.41
  312.2 0.0 reduce-scatter.2.cloned.1.call-update
  312.2 39.5 %reduce-scatter.2.cloned.1.call-done = f32[32,768]{1,0:T(8,128)} async-done(((f32[32,6144]{1,0:T(8,128)}), f32[32,768]{1,0:T(8,128)}) %reduce-scatter.2.cloned.1.call-update) | async-done | bytes 98320 | tf_op jit(solution)/shard_map/reduce_scatter | solution.py:119
  351.7 1.5 dynamic-slice_add_fusion
  (5 shorter events, 0.0 us)
Async XLA Ops:
  6.5 2.6 copy-start
  6.5 77.5 %all-reduce.2.cloned.1.call-start = ((), (), s32[]{:S(2)}) async-start(), calls=%async_computation.3 | async-start | bytes 1572864 | tf_op jit(solution)/shard_map/psum | solution.py:78
  13.5 6.4 %copy-start.3 = (s32[32,2]{0,1:T(2,128)S(1)}, s32[32,2]{0,1:T(2,128)}, u32[]{:S(2)}) copy-start(s32[32,2]{0,1:T(2,128)} %param.26) | copy-start | bytes 772
  13.5 72.0 %copy-start.2 = (f32[6144]{0:T(1024)S(1)}, f32[6144]{0:T(1024)}, u32[]{:S(2)}) copy-start(f32[6144]{0:T(1024)} %param.22) | copy-start | bytes 73732
  86.1 64.7 %slice-start = ((s8[4718592]{0:T(1024)(128)(4,1)}), s8[524288]{0:T(1024)(128)(4,1)S(1)}, s32[]{:S(2)}) async-start(s8[4718592]{0:T(1024)(128)(4,1)} %bitcast.50), calls=%async_computation.5 | async-start | bytes 1048576
  86.6 64.1 %slice-start.1 = ((s8[4718592]{0:T(1024)(128)(4,1)}), s8[4194304]{0:T(1024)(128)(4,1)S(1)}, s32[]{:S(2)}) async-start(s8[4718592]{0:T(1024)(128)(4,1)} %bitcast.50), calls=%async_computation.6 | async-start | bytes 8388608
  148.5 2.2 copy-start.1
  168.1 5.0 %copy-start.4 = (f32[32,2]{0,1:T(2,128)S(1)}, f32[32,2]{0,1:T(2,128)}, u32[]{:S(2)}) copy-start(f32[32,2]{0,1:T(2,128)} %param.27) | copy-start | bytes 772
  168.1 137.3 %all-to-all-start.1 = ((f32[16,24,6144]{2,1,0:T(8,128)}), f32[16,24,6144]{2,1,0:T(8,128)}, u32[]{:S(2)}, u32[]{:S(2)}) async-start(f32[16,24,6144]{2,1,0:T(8,128)} %bitcast.41), calls=%async_computation.1 | async-start | bytes 18874368 | tf_op jit(solution)/shard_map/all_to_all | solution.py:106
  173.0 178.7 %reduce-scatter.2.cloned.1.call-start = ((), (), s32[]{:S(2)}) async-start(), calls=%async_computation.4 | async-start | bytes 884736 | tf_op jit(solution)/shard_map/reduce_scatter | solution.py:119
Sparse Core Ops, SparseCore 0:
  20.0 64.0 all-reduce.1
  312.4 39.3 reduce-scatter.1
where the time goes:
time: 361 us; the launch traced here: 360 us
  waiting for transfers between devices  235 us (65%)
  blocking collectives  61.8 us (17%)
  matrix products  30.5 us (8%)
  between operations  13.6 us (4%)
  other arithmetic  9.87 us (3%)
  starting transfers between devices  4.95 us (1%)
  local copies, waits for them, and re-layouts  4.22 us (1%)
    all_to_all x1, waiting for transfers between devices, layer_block(): lax.all_to_all(produced.reshape(pool_size, capacity, model_width), 'attn'...  132 us
    psum x1, waiting for transfers between devices, layer_block(): full_mid = residual.astype(jnp.float32) + lax.psum(partial_value, 'expert')  63.4 us
    all_to_all x1, blocking collectives, layer_block(): lax.all_to_all(outgoing, 'attn', split_axis=0, concat_axis=0, tiled=True)  61.8 us
    reduce_scatter x1, waiting for transfers between devices, layer_block(): lax.psum_scatter(token_rows, 'expert', scatter_dimension=1, tiled=True)  39.5 us
    dot_general x1, matrix products, layer_block(): produced = jnp.dot(hidden, down_weight, preferred_element_type=jnp.float32)  14 us
  transfers between devices with their start and end apart: 3, of which 3 were waited for; matrix products, arithmetic and copies ran while one was open for 0% of the time, Pallas kernels for 0%

commit v1 on v0

v1 whole, which is shorter than its diff:
```python
import functools
import math

import jax
import jax.numpy as jnp
from jax import lax
from jax.experimental import pallas as pl
from jax.experimental.pallas import tpu as pltpu
from jax.sharding import Mesh, PartitionSpec as P

EXPERTS = 4
CAP = 24
CORES = 2
EPSILON = 1e-05

CHIPS = ("z", "x", "y")
GROUP = ("y", "core")


def attend(queries, new_keys, new_values, key_cache, value_cache, cache_lengths):
    row_count, kv_groups, cache_span, head_width = key_cache.shape
    heads_per = queries.shape[1] // (kv_groups * head_width)
    score_scale = 1.0 / math.sqrt(head_width)
    query_heads = queries.reshape(row_count, kv_groups, heads_per, head_width)
    scores = (
        jnp.einsum("bghd,bgld->bghl", query_heads, key_cache, preferred_element_type=jnp.float32)
        * score_scale
    )
    fresh_scores = (
        jnp.einsum(
            "bghd,bgd->bgh",
            query_heads,
            new_keys.reshape(row_count, kv_groups, head_width),
            preferred_element_type=jnp.float32,
        )
        * score_scale
    )
    visible = (jnp.arange(cache_span)[None, :] < cache_lengths[:, None])[:, None, None, :]
    scores = jnp.where(visible, scores, -jnp.inf)
    largest = jnp.maximum(jnp.max(scores, axis=3), fresh_scores)
    exp_scores = jnp.exp(scores - largest[..., None])
    exp_fresh = jnp.exp(fresh_scores - largest)
    denominator = jnp.sum(exp_scores, axis=3) + exp_fresh
    weights = (exp_scores / denominator[..., None]).astype(jnp.bfloat16)
    weights_new = (exp_fresh / denominator).astype(jnp.bfloat16)
    mixture = jnp.einsum(
        "bghl,bgld->bghd", weights, value_cache, preferred_element_type=jnp.float32
    )
    mixture = mixture + weights_new.astype(jnp.float32)[..., None] * new_values.reshape(
        row_count, kv_groups, 1, head_width
    ).astype(jnp.float32)
    return mixture.reshape(row_count, kv_groups * heads_per * head_width).astype(jnp.bfloat16)


def hidden_kernel(
    core, own, other, gain, gate, up, down, hidden_ref, send_ref, gate_acc, up_acc, squares, hidden
):
    step = pl.program_id(0)
    blocks, cap, width = own.shape[0], own.shape[2], own.shape[3]
    rows = blocks * cap

    @pl.when(step == 0)
    def _():
        gate_acc[...] = jnp.zeros_like(gate_acc)
        up_acc[...] = jnp.zeros_like(up_acc)
        squares[...] = jnp.zeros_like(squares)

    def add_block(source):
        wide = source[...].astype(jnp.float32).reshape(rows, width)
        plain = wide * (1.0 / gain[0])
        squares[...] += jnp.sum(plain * plain, axis=1, keepdims=True)
        block = wide.astype(jnp.bfloat16)
        gate_acc[...] += jnp.dot(block, gate[...], preferred_element_type=jnp.float32)
        up_acc[...] += jnp.dot(block, up[...], preferred_element_type=jnp.float32)

    @pl.when(step < 4)
    def _():
        add_block(own)

    @pl.when((step >= 4) & (step < 8))
    def _():
        add_block(other)

    @pl.when(step == 7)
    def _():
        scale = lax.rsqrt(squares[...] * (1.0 / (8 * width)) + EPSILON)
        gate_sum = gate_acc[...] * scale
        value = (gate_sum / (1.0 + jnp.exp(-gate_sum)) * (up_acc[...] * scale)).astype(jnp.bfloat16)
        hidden[...] = value
        hidden_ref[...] = value

    @pl.when(step >= 8)
    def _():
        out = jnp.dot(hidden[...], down[...], preferred_element_type=jnp.float32)
        send_ref[...] = out.reshape(blocks, 1, cap, width).astype(send_ref.dtype)


def own_kernel(core, hidden, down, out_ref):
    blocks, _, cap, width = out_ref.shape
    out = jnp.dot(hidden[...], down[...], preferred_element_type=jnp.float32)
    out_ref[...] = out.reshape(blocks, 1, cap, width).astype(out_ref.dtype)


def expert_halves(core, own, other, gain, gate, up, down):
    blocks, ys, cap, width = own.shape
    units = gate.shape[1]
    rows = blocks * cap

    def k_block(step, core):
        k = jnp.minimum(step, 7)
        return jnp.where(k < 4, 2 * k + core[0], 2 * (k - 4) + 1 - core[0])

    def n_block(step, core):
        return 2 * jnp.maximum(step - 8, 0) + 1 - core[0]

    return pl.pallas_call(
        hidden_kernel,
        grid_spec=pltpu.PrefetchScalarGridSpec(
            num_scalar_prefetch=1,
            grid=(12,),
            in_specs=[
                pl.BlockSpec((blocks, 1, cap, width), lambda i, c: (0, jnp.minimum(i, 3), 0, 0)),
                pl.BlockSpec((blocks, 1, cap, width), lambda i, c: (0, jnp.clip(i - 4, 0, 3), 0, 0)),
                pl.BlockSpec((1, 1, width), lambda i, c: (k_block(i, c), 0, 0)),
                pl.BlockSpec((width, units), lambda i, c: (k_block(i, c), 0)),
                pl.BlockSpec((width, units), lambda i, c: (k_block(i, c), 0)),
                pl.BlockSpec((units, width), lambda i, c: (0, n_block(i, c))),
            ],
            out_specs=[
                pl.BlockSpec((rows, units), lambda i, c: (0, 0)),
                pl.BlockSpec((blocks, 1, cap, width), lambda i, c: (0, jnp.maximum(i - 8, 0), 0, 0)),
            ],
            scratch_shapes=[
                pltpu.VMEM((rows, units), jnp.float32),
                pltpu.VMEM((rows, units), jnp.float32),
                pltpu.VMEM((rows, 1), jnp.float32),
                pltpu.VMEM((rows, units), jnp.bfloat16),
            ],
        ),
        out_shape=[
            jax.ShapeDtypeStruct((rows, units), jnp.bfloat16),
            jax.ShapeDtypeStruct((blocks, ys, cap, width), jnp.bfloat16),
        ],
        compiler_params=pltpu.CompilerParams(vmem_limit_bytes=40 * 2**20),
        cost_estimate=pl.CostEstimate(
            flops=5 * rows * units * 8 * width, bytes_accessed=20 * 2**20, transcendentals=0
        ),
        name="experts_in",
    )(core, own, other, gain, gate, up, down)


def expert_own(core, hidden, down, blocks, cap, width):
    rows, units = hidden.shape
    return pl.pallas_call(
        own_kernel,
        grid_spec=pltpu.PrefetchScalarGridSpec(
            num_scalar_prefetch=1,
            grid=(4,),
            in_specs=[
                pl.BlockSpec((rows, units), lambda i, c: (0, 0)),
                pl.BlockSpec((units, width), lambda i, c: (0, 2 * i + c[0])),
            ],
            out_specs=pl.BlockSpec((blocks, 1, cap, width), lambda i, c: (0, i, 0, 0)),
        ),
        out_shape=jax.ShapeDtypeStruct((blocks, 4, cap, width), jnp.bfloat16),
        compiler_params=pltpu.CompilerParams(vmem_limit_bytes=32 * 2**20),
        cost_estimate=pl.CostEstimate(
            flops=rows * units * 8 * width, bytes_accessed=5 * 2**20, transcendentals=0
        ),
        name="experts_own",
    )(core, hidden, down)


def swap(value):
    return lax.ppermute(value, "core", [(0, 1), (1, 0)])


def layer_block(
    residual,
    queries,
    new_keys,
    new_values,
    key_cache,
    value_cache,
    cache_lengths,
    out_weight,
    norm_gain,
    gate_weight,
    up_weight,
    down_weight,
    routes,
    route_gates,
):
    rows, width = residual.shape
    ways = lax.axis_size("y") * lax.axis_size("core")
    share = width // ways
    planes = lax.axis_size("z")
    chips = lax.axis_size("x") * lax.axis_size("y")
    core = lax.axis_index("core")
    column = lax.axis_index("y") * CORES + core

    attended = attend(queries, new_keys, new_values, key_cache, value_cache, cache_lengths)
    partial = jnp.dot(attended, out_weight, preferred_element_type=jnp.float32)
    pieces = partial.astype(jnp.bfloat16).reshape(rows, ways, share).transpose(1, 0, 2)
    pieces = lax.all_to_all(pieces, GROUP, split_axis=0, concat_axis=0, tiled=True)
    start = column * share
    middle = lax.dynamic_slice_in_dim(residual, start, share, 1).astype(jnp.float32)
    middle = middle + jnp.sum(pieces.astype(jnp.float32), axis=0)
    gain = lax.dynamic_slice_in_dim(norm_gain, start, share, 0)
    gained = (middle * gain).astype(jnp.bfloat16)

    flat_routes = routes.reshape(-1)
    one_hot = (flat_routes[:, None] == jnp.arange(EXPERTS)[None, :]).astype(jnp.int32)
    slot_rank = jnp.sum((jnp.cumsum(one_hot, axis=0) - one_hot) * one_hot, axis=1)
    slot_index = flat_routes * CAP + slot_rank
    slot_match = (slot_index[:, None] == jnp.arange(EXPERTS * CAP)[None, :]).reshape(
        rows, 2, EXPERTS * CAP
    )
    chosen = jnp.any(slot_match, axis=1).astype(jnp.bfloat16)
    blend = jnp.sum(slot_match.astype(jnp.float32) * route_gates[:, :, None], axis=1)

    outgoing = jnp.einsum("ts,tc->sc", chosen, gained, preferred_element_type=jnp.float32)
    outgoing = outgoing.astype(jnp.bfloat16).reshape(EXPERTS, 1, CAP, share)
    outgoing = jnp.broadcast_to(outgoing, (EXPERTS, chips, CAP, share))
    own = lax.all_to_all(
        outgoing.reshape(EXPERTS * chips, CAP, share), CHIPS, split_axis=0, concat_axis=0, tiled=True
    )
    other = swap(own)

    core_index = core.astype(jnp.int32).reshape(1)
    shape = (planes * lax.axis_size("x"), lax.axis_size("y"), CAP, share)
    hidden, send = expert_halves(
        core_index,
        own.reshape(shape),
        other.reshape(shape),
        norm_gain.reshape(ways, 1, share),
        gate_weight,
        up_weight,
        down_weight,
    )
    given = swap(send)
    kept = expert_own(core_index, hidden, down_weight, shape[0], CAP, share)
    total = (kept.astype(jnp.float32) + given.astype(jnp.float32)).astype(jnp.bfloat16)
    returned = lax.all_to_all(
        total.reshape(EXPERTS * chips, CAP, share), CHIPS, split_axis=0, concat_axis=0, tiled=True
    )
    merged = jnp.sum(
        returned.reshape(EXPERTS, chips, CAP, share).astype(jnp.float32), axis=1
    ).reshape(EXPERTS * CAP, share)
    return middle + jnp.dot(blend, merged, precision=lax.Precision.HIGHEST)


def solution(mesh):
    fine = Mesh(mesh.devices.reshape(4, 4, 4, 2), ("z", "x", "y", "core"))
    attn, expert = ("z", "x"), ("y", "core")
    every = attn + expert
    in_specs = (
        P(attn, None),
        P(attn, expert),
        P(attn, expert),
        P(attn, expert),
        P(attn, expert, None, None),
        P(attn, expert, None, None),
        P(attn),
        P(expert, None),
        P(),
        P(None, every),
        P(None, every),
        P(every, None),
        P(attn, None),
        P(attn, None),
    )
    return jax.shard_map(
        layer_block, mesh=fine, in_specs=in_specs, out_specs=P(attn, expert), check_vma=False
    )
```

time: 361 us -> 137 us (0.38)
  waiting for transfers between devices: 235 us -> 47.4 us
  matrix products: 30.5 us -> 10.6 us
  blocking collectives: 61.8 us -> 42 us
  Pallas kernels: 0 us -> 15.2 us
  between operations: 13.6 us -> 0.19 us
  starting transfers between devices: 4.95 us -> 10.5 us
  other arithmetic: 9.87 us -> 5.83 us
    all_to_all x1 -> x2, waiting for transfers between devices: 132 us -> 40.6 us  [the longest x1 32.6 us: layer_block(): lax.all_to_all(total.reshape(EXPERTS * chips, CAP, share), CHIPS, split_a...]
    psum x1 -> x0, waiting for transfers between devices: 63.4 us -> none  [layer_block(): full_mid = residual.astype(jnp.float32) + lax.psum(partial_value, 'expert')]
    reduce_scatter x1 -> x0, waiting for transfers between devices: 39.5 us -> none  [layer_block(): lax.psum_scatter(token_rows, 'expert', scatter_dimension=1, tiled=True)]
    all_to_all x1, blocking collectives: 61.8 us -> 42 us  [layer_block(): lax.all_to_all(outgoing.reshape(EXPERTS * chips, CAP, share), CHIPS, spli...]
    dot_general x5 -> x3, matrix products: 26.4 us -> 8.19 us  [the longest x1 5.41 us: layer_block(): partial = jnp.dot(attended, out_weight, preferred_element_type=jnp.float32)]
    pallas_call x0 -> x2, Pallas kernels: none -> 15.2 us  [the longest x1 13 us: expert_halves(): pl.pallas_call(hidden_kernel, grid_spec=pltpu.PrefetchScalarGridSpec(num_...]
    ppermute x0 -> x2, waiting for transfers between devices: none -> 6.73 us  [swap(): return lax.ppermute(value, 'core', [(0, 1), (1, 0)])]
    all_to_all x1 -> x2, starting transfers between devices: 4.91 us -> 10.3 us  [the longest x1 5.73 us: layer_block(): lax.all_to_all(total.reshape(EXPERTS * chips, CAP, share), CHIPS, split_a...]
  transfers between devices with their start and end apart: 3 -> 4, of which waited for: 3 -> 4; matrix products, arithmetic and copies ran while one was open for 0% -> 1% of each run, Pallas kernels for 0% -> 2%
where the time goes in v1:
time: 137 us
  waiting for transfers between devices  47.4 us (35%)
  blocking collectives  42 us (31%)
  Pallas kernels  15.2 us (11%)
  matrix products  10.6 us (8%)
  starting transfers between devices  10.5 us (8%)
  other arithmetic  5.83 us (4%)
  local copies, waits for them, and re-layouts  4.94 us (4%)
    all_to_all x1, blocking collectives, layer_block(): lax.all_to_all(outgoing.reshape(EXPERTS * chips, CAP, share), CHIPS, spli...  42 us
    all_to_all x1, waiting for transfers between devices, layer_block(): lax.all_to_all(total.reshape(EXPERTS * chips, CAP, share), CHIPS, split_a...  32.6 us
    pallas_call x1, Pallas kernels, expert_halves(): pl.pallas_call(hidden_kernel, grid_spec=pltpu.PrefetchScalarGridSpec(num_...  13 us
    all_to_all x1, waiting for transfers between devices, layer_block(): lax.all_to_all(pieces, GROUP, split_axis=0, concat_axis=0, tiled=True)  8.01 us
    ppermute x2, waiting for transfers between devices, swap(): return lax.ppermute(value, 'core', [(0, 1), (1, 0)])  6.73 us
    all_to_all x1, starting transfers between devices, layer_block(): lax.all_to_all(total.reshape(EXPERTS * chips, CAP, share), CHIPS, split_a...  5.73 us
    dot_general x1, matrix products, layer_block(): partial = jnp.dot(attended, out_weight, preferred_element_type=jnp.float32)  5.41 us
    all_to_all x1, starting transfers between devices, layer_block(): lax.all_to_all(pieces, GROUP, split_axis=0, concat_axis=0, tiled=True)  4.55 us
  transfers between devices with their start and end apart: 4, of which 4 were waited for; matrix products, arithmetic and copies ran while one was open for 1% of the time, Pallas kernels for 2%

profile of v1, /device:TPU:0, one launch (start us, length us, event | category | flops | bytes accessed | tf_op | source)
XLA Modules:
  0.0 136.7 jit_solution(11675422232984737002)
XLA Ops:
  0.0 0.0 copy-start
  0.0 1.0 reshape.132
  1.0 0.0 copy-start.6
  1.0 0.9 iota_compare_fusion
  1.9 0.9 fusion.25
  2.8 0.0 copy-done
  2.8 1.0 fusion.30
  3.8 0.2 fusion.16
  4.1 0.0 copy-done.3
  4.1 0.0 copy-done.6
  4.1 0.6 fusion.13
  4.7 0.0 copy-start.4
  4.7 0.0 copy-start.2
  4.7 5.4 %convolution_convert_fusion = bf16[32,6144]{1,0:T(8,128)(2,1)S(1)} fusion(bf16[768,6144]{1,0:T(8,128)(2,1)} %param.21, bf16[4,8,6,128]{3,2,1,0:T(8,128)(2,1)S(1)} %bitcast.57), kind=kOutput, calls=%fused_computation | convolution fusion | flops 302186496 | bytes 9879552 | tf_op jit(solution)/shard_map/dot_general | solution.py:203
  10.1 0.8 copy.47
  10.9 4.6 %all-to-all-start = ((bf16[8,32,768]{2,1,0:T(8,128)(2,1)}), bf16[8,32,768]{2,1,0:T(8,128)(2,1)S(1)}, u32[]{:S(2)}, u32[]{:S(2)}) async-start(bf16[8,32,768]{2,1,0:T(8,128)(2,1)} %bitcast.46), calls=%async_computation | async-start | bytes 786432 | tf_op jit(solution)/shard_map/all_to_all | solution.py:205
  15.5 0.0 copy-done.4
  15.5 0.1 copy.34
  15.6 0.1 eq.29
  15.7 0.1 fusion.24
  15.7 0.1 reduce_window_sum.11
  15.8 0.2 select_reduce_fusion.1
  16.0 0.1 reduce_sum.50
  16.1 0.1 copy.35
  16.2 0.0 copy-done.2
  16.2 0.1 dynamic_slice.7
  16.3 0.1 fusion.23
  16.4 8.0 %all-to-all-done = bf16[8,32,768]{2,1,0:T(8,128)(2,1)S(1)} async-done(((bf16[8,32,768]{2,1,0:T(8,128)(2,1)}), bf16[8,32,768]{2,1,0:T(8,128)(2,1)S(1)}, u32[]{:S(2)}, u32[]{:S(2)}) %all-to-all-start) | async-done | bytes 393248 | tf_op jit(solution)/shard_map/all_to_all | solution.py:205
  24.4 0.1 convert_reduce_fusion.1
  24.5 1.1 convolution_convert_fusion.1
  25.5 0.2 broadcast_in_dim.19
  25.7 42.0 %all_to_all.15 = bf16[64,24,768]{2,1,0:T(8,128)(2,1)S(1)} all-to-all(bf16[64,24,768]{2,1,0:T(8,128)(2,1)S(1)} %bitcast.53), channel_id=1, replica_groups=mesh['z'=4,'x'=4,'y'=4,'core'=2] {'z','x','y'}, dimensions={0} | all-to-all | bytes 4718592 | tf_op jit(solution)/shard_map/all_to_all | solution.py:225
  67.7 0.0 collective-permute-start
  67.7 4.5 %collective-permute-done = bf16[64,24,768]{2,1,0:T(8,128)(2,1)S(1)} collective-permute-done((bf16[64,24,768]{2,1,0:T(8,128)(2,1)S(1)}, bf16[64,24,768]{2,1,0:T(8,128)(2,1)S(1)}, u32[]{:S(2)}, u32[]{:S(2)}) %collective-permute-start) | collective-permute-done | bytes 2359328 | tf_op jit(solution)/shard_map/ppermute | solution.py:175
  72.2 2.5 %copy-done.1 = bf16[6144,384]{1,0:T(8,128)(2,1)S(1)} copy-done((bf16[6144,384]{1,0:T(8,128)(2,1)S(1)}, bf16[6144,384]{1,0:T(8,128)(2,1)}, u32[]{:S(2)}) %copy-start.1) | copy-done | bytes 4718616
  74.7 13.0 %experts_in.1 = (bf16[384,384]{1,0:T(8,128)(2,1)S(1)}, bf16[16,4,24,768]{3,2,1,0:T(8,128)(2,1)S(1)}) custom-call(s32[1]{0:T(128)} %bitcast.6.core, bf16[16,4,24,768]{3,2,1,0:T(8,128)(2,1)S(1)} %bitcast.49, bf16[16,4,24,768]{3,2,1,0:T(8,128)(2,1)S(1)} %bitcast.50, f32[8,1,768]{2,1,0:T(1,128)S(1)} %bitcast.51, bf16[6144,384]{1,0:T(8,128)(2,1)S(1)} %copy-done.1, ...), custom_call_target="tpu_custom_call" | custom-call | flops 4529848320 | bytes 20971520 | tf_op jit(solution)/shard_map/experts_in/pallas_call | solution.py:116
  87.7 0.2 collective-permute-start.1
  88.0 0.0 slice-done
  88.0 0.0 slice-done.1
  88.0 2.2 %experts_own.1 = bf16[16,4,24,768]{3,2,1,0:T(8,128)(2,1)S(1)} custom-call(s32[1]{0:T(128)} %bitcast.6.core, bf16[384,384]{1,0:T(8,128)(2,1)S(1)} %get-tuple-element.7.hidden, bf16[384,6144]{1,0:T(8,128)(2,1)S(1)} %bitcast.48), custom_call_target="tpu_custom_call" | custom-call | flops 905969664 | bytes 5242880 | tf_op jit(solution)/shard_map/experts_own/pallas_call | solution.py:154
  90.2 2.2 %collective-permute-done.1 = bf16[16,4,24,768]{3,2,1,0:T(8,128)(2,1)S(1)} collective-permute-done((bf16[16,4,24,768]{3,2,1,0:T(8,128)(2,1)S(1)}, bf16[16,4,24,768]{3,2,1,0:T(8,128)(2,1)S(1)}, u32[]{:S(2)}, u32[]{:S(2)}) %collective-permute-start.1) | collective-permute-done | bytes 2359328 | tf_op jit(solution)/shard_map/ppermute | solution.py:175
  92.4 2.1 %add_convert_fusion = bf16[16,4,24,768]{3,2,1,0:T(8,128)(2,1)} fusion(bf16[16,4,24,768]{3,2,1,0:T(8,128)(2,1)S(1)} %collective-permute-done.1, bf16[16,4,24,768]{3,2,1,0:T(8,128)(2,1)S(1)} %experts_own.1), kind=kLoop, calls=%fused_computation.2 | loop fusion | flops 4718592 | bytes 7077888 | tf_op jit(solution)/shard_map/convert_element_type | solution.py:243
  94.5 5.7 %all-to-all-start.2 = ((bf16[64,24,768]{2,1,0:T(8,128)(2,1)}), bf16[64,24,768]{2,1,0:T(8,128)(2,1)}, u32[]{:S(2)}, u32[]{:S(2)}) async-start(bf16[64,24,768]{2,1,0:T(8,128)(2,1)} %bitcast.52), calls=%async_computation.2 | async-start | bytes 4718592 | tf_op jit(solution)/shard_map/all_to_all | solution.py:244
  100.2 0.0 copy-done.5
  100.2 0.1 select_reduce_fusion
  100.3 32.6 %all-to-all-done.2 = bf16[64,24,768]{2,1,0:T(8,128)(2,1)} async-done(((bf16[64,24,768]{2,1,0:T(8,128)(2,1)}), bf16[64,24,768]{2,1,0:T(8,128)(2,1)}, u32[]{:S(2)}, u32[]{:S(2)}) %all-to-all-start.2) | async-done | bytes 2359328 | tf_op jit(solution)/shard_map/all_to_all | solution.py:244
  132.9 2.0 %convert_reduce_fusion = f32[4,24,768]{2,1,0:T(8,128)S(1)} fusion(bf16[64,24,768]{2,1,0:T(8,128)(2,1)} %all-to-all-done.2), kind=kLoop, calls=%fused_computation.1 | loop fusion | flops 2285568 | bytes 2654208 | tf_op jit(solution)/shard_map/reduce_sum | solution.py:247
  135.0 1.7 %convolution_add_fusion = f32[32,768]{1,0:T(8,128)} fusion(f32[32,96]{1,0:T(8,128)S(1)} %select_reduce_fusion, f32[96,768]{1,0:T(8,128)S(1)} %bitcast.55, f32[32,768]{1,0:T(8,128)S(1)} %convert_reduce_fusion.1, bf16[32,6144]{1,0:T(8,128)(2,1)} %param.14, s32[]{:T(128)S(6)} %select_n.9), kind=kOutput, calls=%fused_computation.12 | convolution fusion | flops 28385280 | bytes 552964 | tf_op jit(solution)/shard_map/dot_general | solution.py:250
  (10 shorter events, 0.0 us)
Async XLA Ops:
  0.0 2.8 %copy-start = (bf16[32,1,320,128]{3,2,1,0:T(8,128)(2,1)S(1)}, bf16[32,1,320,128]{3,2,1,0:T(8,128)(2,1)}, u32[]{:S(2)}) copy-start(bf16[32,1,320,128]{3,2,1,0:T(8,128)(2,1)} %param.18) | copy-start | bytes 7864324
  0.0 4.1 %copy-start.3 = (bf16[32,128]{1,0:T(8,128)(2,1)S(1)}, bf16[32,128]{1,0:T(8,128)(2,1)}, u32[]{:S(2)}) copy-start(bf16[32,128]{1,0:T(8,128)(2,1)} %param.17) | copy-start | bytes 24580
  1.0 3.0 %copy-start.6 = (bf16[32,1,320,128]{3,2,1,0:T(8,128)(2,1)S(1)}, bf16[32,1,320,128]{3,2,1,0:T(8,128)(2,1)}, u32[]{:S(2)}) copy-start(bf16[32,1,320,128]{3,2,1,0:T(8,128)(2,1)} %param.19) | copy-start | bytes 7864324
  4.7 10.8 %copy-start.4 = (s32[32,2]{0,1:T(2,128)S(1)}, s32[32,2]{0,1:T(2,128)}, u32[]{:S(2)}) copy-start(s32[32,2]{0,1:T(2,128)} %param.26) | copy-start | bytes 772
  4.7 11.5 %copy-start.2 = (f32[6144]{0:T(1024)S(1)}, f32[6144]{0:T(1024)}, u32[]{:S(2)}) copy-start(f32[6144]{0:T(1024)} %param.22) | copy-start | bytes 73732
  10.9 13.5 %all-to-all-start = ((bf16[8,32,768]{2,1,0:T(8,128)(2,1)}), bf16[8,32,768]{2,1,0:T(8,128)(2,1)S(1)}, u32[]{:S(2)}, u32[]{:S(2)}) async-start(bf16[8,32,768]{2,1,0:T(8,128)(2,1)} %bitcast.46), calls=%async_computation | async-start | bytes 786432 | tf_op jit(solution)/shard_map/all_to_all | solution.py:205
  67.7 4.5 %collective-permute-start = (bf16[64,24,768]{2,1,0:T(8,128)(2,1)S(1)}, bf16[64,24,768]{2,1,0:T(8,128)(2,1)S(1)}, u32[]{:S(2)}, u32[]{:S(2)}) collective-permute-start(bf16[64,24,768]{2,1,0:T(8,128)(2,1)S(1)} %all_to_all.15), channel_id=1, source_target_pairs={{0,1},{1,0},{2,3},{3,2},{4,5},{5,4},{6,7},{7,6},{8,9},{9,8},{10,11... | collective-permute-start | bytes 7077896 | tf_op jit(solution)/shard_map/ppermute | solution.py:175
  72.2 15.7 %slice-start = ((s8[4718592]{0:T(1024)(128)(4,1)}), s8[4194304]{0:T(1024)(128)(4,1)S(1)}, s32[]{:S(2)}) async-start(s8[4718592]{0:T(1024)(128)(4,1)} %bitcast.47), calls=%async_computation.3 | async-start | bytes 8388608
  72.2 2.5 %copy-start.1 = (bf16[6144,384]{1,0:T(8,128)(2,1)S(1)}, bf16[6144,384]{1,0:T(8,128)(2,1)}, u32[]{:S(2)}) copy-start(bf16[6144,384]{1,0:T(8,128)(2,1)} %gate.1) | copy-start | bytes 14155780
  74.7 13.2 %slice-start.1 = ((s8[4718592]{0:T(1024)(128)(4,1)}), s8[524288]{0:T(1024)(128)(4,1)S(1)}, s32[]{:S(2)}) async-start(s8[4718592]{0:T(1024)(128)(4,1)} %bitcast.47), calls=%async_computation.4 | async-start | bytes 1048576
  87.7 4.6 %collective-permute-start.1 = (bf16[16,4,24,768]{3,2,1,0:T(8,128)(2,1)S(1)}, bf16[16,4,24,768]{3,2,1,0:T(8,128)(2,1)S(1)}, u32[]{:S(2)}, u32[]{:S(2)}) collective-permute-start(bf16[16,4,24,768]{3,2,1,0:T(8,128)(2,1)S(1)} %get-tuple-element.8), channel_id=1, source_target_pairs={{0,1},{1,0},{2,3},{3,2},{4,5},{5,4},{6,7},{7,6},{8,9},{9,8},{10,11... | collective-permute-start | bytes 7077896 | tf_op jit(solution)/shard_map/ppermute | solution.py:175
  94.5 5.7 %copy-start.5 = (f32[32,2]{0,1:T(2,128)S(1)}, f32[32,2]{0,1:T(2,128)}, u32[]{:S(2)}) copy-start(f32[32,2]{0,1:T(2,128)} %param.27) | copy-start | bytes 772
  94.5 38.5 %all-to-all-start.2 = ((bf16[64,24,768]{2,1,0:T(8,128)(2,1)}), bf16[64,24,768]{2,1,0:T(8,128)(2,1)}, u32[]{:S(2)}, u32[]{:S(2)}) async-start(bf16[64,24,768]{2,1,0:T(8,128)(2,1)} %bitcast.52), calls=%async_computation.2 | async-start | bytes 4718592 | tf_op jit(solution)/shard_map/all_to_all | solution.py:244

commit v2 on v1

v2 whole, which is shorter than its diff:
```python
import functools
import math

import jax
import jax.numpy as jnp
from jax import lax
from jax.experimental import pallas as pl
from jax.experimental.pallas import tpu as pltpu
from jax.sharding import Mesh, PartitionSpec as P

EXPERTS = 4
CAP = 24
CORES = 2
EPSILON = 1e-05

CHIPS = ("z", "x", "y")
GROUP = ("y", "core")


PART = 8


def in_hbm(*arrays):
    return tuple(pltpu.with_memory_space_constraint(array, pltpu.HBM) for array in arrays)


def attend_kernel(
    place, lengths, queries, new_keys, new_values, keys, values, out_weight,
    sent_ref, kept_ref,
    length_buf, query_buf, new_key_buf, new_value_buf, key_buf, value_buf, weight_buf, sems,
):
    rows, head_width = new_keys.shape
    heads = queries.shape[1] // head_width
    _, ys, _, width = weight_buf.shape
    span = keys.shape[2]
    parts = rows // PART
    scale = 1.0 / math.sqrt(head_width)

    copies = [
        (lengths, length_buf),
        (queries, query_buf),
        (new_keys, new_key_buf),
        (new_values, new_value_buf),
    ]
    base = len(copies)
    for cache, target in ((keys, key_buf), (values, value_buf)):
        for p in range(parts):
            some = pl.ds(p * PART, PART)
            copies.append((cache.at[some, 0], target.at[some]))
    for half, side in enumerate((1 - place[0], place[0])):
        for step in range(ys):
            block = 2 * lax.rem(place[1] + step, ys) + side
            columns = pl.ds(pl.multiple_of(block * width, width), width)
            copies.append((out_weight.at[:, columns], weight_buf.at[half, step]))
    copies = [
        pltpu.make_async_copy(source, target, sems.at[i]) for i, (source, target) in enumerate(copies)
    ]
    for copy in copies:
        copy.start()
    for copy in copies[:base]:
        copy.wait()
    copies = copies[base:]

    query_heads = query_buf[...].astype(jnp.float32).reshape(rows, heads, head_width)
    new_key = new_key_buf[...].astype(jnp.float32).reshape(rows, 1, head_width)
    new_value = new_value_buf[...].astype(jnp.float32).reshape(rows, 1, head_width)
    fresh = jnp.sum(query_heads * new_key, axis=2, keepdims=True) * scale
    query_heads = query_heads.astype(jnp.bfloat16)
    position = lax.broadcasted_iota(jnp.int32, (heads, span), 1)
    scores = []
    for p in range(parts):
        copies[p].wait()
        some = slice(p * PART, (p + 1) * PART)
        product = jnp.einsum(
            "bhd,bld->bhl", query_heads[some], key_buf[some], preferred_element_type=jnp.float32
        )
        for i in range(PART):
            visible = position < length_buf[0, p * PART + i]
            scores.append(jnp.where(visible, product[i] * scale, -jnp.inf))
    scores = jnp.stack(scores)
    largest = jnp.maximum(jnp.max(scores, axis=2, keepdims=True), fresh)
    exp_scores = jnp.exp(scores - largest)
    exp_fresh = jnp.exp(fresh - largest)
    inverse = 1.0 / (jnp.sum(exp_scores, axis=2, keepdims=True) + exp_fresh)
    weights = (exp_scores * inverse).astype(jnp.bfloat16)
    weights_new = (exp_fresh * inverse).astype(jnp.bfloat16).astype(jnp.float32)
    attended = []
    for p in range(parts):
        copies[parts + p].wait()
        some = slice(p * PART, (p + 1) * PART)
        mixture = jnp.einsum(
            "bhl,bld->bhd", weights[some], value_buf[some], preferred_element_type=jnp.float32
        )
        attended.append(mixture + weights_new[some] * new_value[some])
    attended = jnp.concatenate(attended, axis=0).reshape(rows, heads * head_width)
    attended = attended.astype(jnp.bfloat16)
    for half, target in enumerate((sent_ref, kept_ref)):
        for y in range(ys):
            copies[2 * parts + half * ys + y].wait()
            out = jnp.dot(attended, weight_buf[half, y], preferred_element_type=jnp.float32)
            target[y] = out.astype(target.dtype)


def attend(place, lengths, queries, new_keys, new_values, keys, values, out_weight):
    rows, span, head_width = keys.shape[0], keys.shape[2], keys.shape[3]
    ys, width = 4, queries.shape[1]
    scalars = pl.BlockSpec(memory_space=pltpu.SMEM)
    inside = pl.BlockSpec(memory_space=pltpu.VMEM)
    outside = pl.BlockSpec(memory_space=pltpu.HBM)
    return pl.pallas_call(
        attend_kernel,
        in_specs=[scalars] + [outside] * 7,
        out_specs=[inside] * 2,
        out_shape=[
            jax.ShapeDtypeStruct((ys, rows, width), jnp.bfloat16),
            jax.ShapeDtypeStruct((ys, rows, width), jnp.float32),
        ],
        scratch_shapes=[
            pltpu.SMEM((1, rows), jnp.int32),
            pltpu.VMEM((rows, width), jnp.bfloat16),
            pltpu.VMEM((rows, head_width), jnp.bfloat16),
            pltpu.VMEM((rows, head_width), jnp.bfloat16),
            pltpu.VMEM((rows, span, head_width), jnp.bfloat16),
            pltpu.VMEM((rows, span, head_width), jnp.bfloat16),
            pltpu.VMEM((2, ys, width, width), jnp.bfloat16),
            pltpu.SemaphoreType.DMA((4 + 2 * rows // PART + 2 * ys,)),
        ],
        compiler_params=pltpu.CompilerParams(vmem_limit_bytes=32 * 2**20),
        cost_estimate=pl.CostEstimate(
            flops=rows * width * width * 8, bytes_accessed=15 * 2**20, transcendentals=0
        ),
        name="attend",
    )(place, *in_hbm(lengths, queries, new_keys, new_values, keys, values, out_weight))


def gate_up_copies(side, gate, up, target, sems):
    ys, width, units = target.shape[0], target.shape[1], gate.shape[1]
    copies = []
    for y in range(ys):
        rows = pl.ds(pl.multiple_of((2 * y + side) * width, width), width)
        copies.append((gate.at[rows, :], target.at[y, :, pl.ds(0, units)]))
        copies.append((up.at[rows, :], target.at[y, :, pl.ds(units, units)]))
    return [pltpu.make_async_copy(s, t, sems.at[i]) for i, (s, t) in enumerate(copies)]


def load_kernel(core, gate, up, own_weight, other_weight, sems):
    copies = gate_up_copies(core[0], gate, up, own_weight, sems.at[0])
    copies += gate_up_copies(1 - core[0], gate, up, other_weight, sems.at[1])
    for copy in copies:
        copy.start()
    for copy in copies:
        copy.wait()


def load_weights(core, gate, up):
    ys, width, units = 4, 768, gate.shape[1]
    inside = pl.BlockSpec(memory_space=pltpu.VMEM)
    outside = pl.BlockSpec(memory_space=pltpu.HBM)
    return pl.pallas_call(
        load_kernel,
        in_specs=[pl.BlockSpec(memory_space=pltpu.SMEM)] + [outside] * 2,
        out_specs=[inside] * 2,
        out_shape=[jax.ShapeDtypeStruct((ys, width, 2 * units), jnp.bfloat16)] * 2,
        scratch_shapes=[pltpu.SemaphoreType.DMA((2, 2 * ys))],
        compiler_params=pltpu.CompilerParams(vmem_limit_bytes=16 * 2**20),
        cost_estimate=pl.CostEstimate(flops=0, bytes_accessed=19 * 2**20, transcendentals=0),
        name="load_weights",
    )(core, *in_hbm(gate, up))


def down_copies(side, down, down_other, target, sems):
    ys, width, units = target.shape[0], target.shape[2], down.shape[0]
    copies = []
    for y in range(ys):
        columns = pl.ds(pl.multiple_of((2 * y + side) * width, width), width)
        copies.append((down.at[:, columns], target.at[y, pl.ds(0, units), :]))
        copies.append((down_other.at[:, columns], target.at[y, pl.ds(units, units), :]))
    return [pltpu.make_async_copy(s, t, sems.at[i]) for i, (s, t) in enumerate(copies)]


def add_products(side, source, gain, weight, total, squares):
    blocks, ys, cap, width = source.shape
    rows = blocks * cap
    for y in range(ys):
        wide = source[:, y].astype(jnp.float32).reshape(rows, width)
        inverse = 1.0 / gain[pl.ds(2 * y + side, 1), :]
        parts = wide * wide * (inverse * inverse)
        step = parts[:, 0:128]
        for j in range(1, width // 128):
            step = step + parts[:, j * 128 : (j + 1) * 128]
        product = jnp.dot(wide.astype(jnp.bfloat16), weight[y], preferred_element_type=jnp.float32)
        if total is None:
            total, squares = product, step
        else:
            total, squares = total + product, squares + step
    return total, squares


def first_kernel(
    core, own, gain, weight, down, down_other, total_ref, squares_ref, out_weight, sems
):
    copies = down_copies(core[0], down, down_other, out_weight, sems)
    for copy in copies:
        copy.start()
    total, squares = add_products(core[0], own, gain, weight, None, None)
    total_ref[...] = total
    squares_ref[...] = squares
    for copy in copies:
        copy.wait()


def second_kernel(core, other, gain, weight, total_ref, squares_ref, hidden_ref):
    ys, width = other.shape[1], other.shape[3]
    total, squares = add_products(
        1 - core[0], other, gain, weight, total_ref[...], squares_ref[...]
    )
    mean = jnp.sum(squares, axis=1, keepdims=True) * (1.0 / (CORES * ys * width))
    total = total * lax.rsqrt(mean + EPSILON)
    units = total.shape[1] // 2
    gate_sum, up_sum = total[:, :units], total[:, units:]
    hidden_ref[...] = (gate_sum / (1.0 + jnp.exp(-gate_sum)) * up_sum).astype(jnp.bfloat16)


def out_kernel(hidden, hidden_other, weight, out_ref):
    blocks, _, cap, width = out_ref.shape
    units = hidden.shape[1]
    out = jnp.dot(hidden[...], weight[0, :units], preferred_element_type=jnp.float32)
    out += jnp.dot(hidden_other[...], weight[0, units:], preferred_element_type=jnp.float32)
    out_ref[...] = out.reshape(blocks, 1, cap, width).astype(out_ref.dtype)


def experts_first(core, own, gain, weight, down, down_other):
    blocks, ys, cap, width = own.shape
    rows, units = blocks * cap, down.shape[0]
    inside = pl.BlockSpec(memory_space=pltpu.VMEM)
    outside = pl.BlockSpec(memory_space=pltpu.HBM)
    return pl.pallas_call(
        first_kernel,
        in_specs=[pl.BlockSpec(memory_space=pltpu.SMEM)] + [inside] * 3 + [outside, pl.BlockSpec(memory_space=pl.ANY)],
        out_specs=[inside] * 3,
        out_shape=[
            jax.ShapeDtypeStruct((rows, 2 * units), jnp.float32),
            jax.ShapeDtypeStruct((rows, 128), jnp.float32),
            jax.ShapeDtypeStruct((ys, 2 * units, width), jnp.bfloat16),
        ],
        scratch_shapes=[pltpu.SemaphoreType.DMA((2 * ys,))],
        compiler_params=pltpu.CompilerParams(vmem_limit_bytes=16 * 2**20),
        cost_estimate=pl.CostEstimate(
            flops=4 * rows * units * ys * width, bytes_accessed=12 * 2**20, transcendentals=0
        ),
        name="experts_first",
    )(core, own, gain, weight, *in_hbm(down), down_other)


def experts_second(core, other, gain, weight, total, squares):
    rows, units = total.shape[0], total.shape[1] // 2
    ys, width = weight.shape[0], weight.shape[1]
    inside = pl.BlockSpec(memory_space=pltpu.VMEM)
    return pl.pallas_call(
        second_kernel,
        in_specs=[pl.BlockSpec(memory_space=pltpu.SMEM)] + [inside] * 5,
        out_specs=inside,
        out_shape=jax.ShapeDtypeStruct((rows, units), jnp.bfloat16),
        compiler_params=pltpu.CompilerParams(vmem_limit_bytes=16 * 2**20),
        cost_estimate=pl.CostEstimate(
            flops=4 * rows * units * ys * width, bytes_accessed=12 * 2**20, transcendentals=0
        ),
        name="experts_second",
    )(core, pltpu.with_memory_space_constraint(other, pltpu.VMEM), gain, weight, total, squares)


def experts_out(hidden, hidden_other, weight, blocks):
    rows, units = hidden.shape
    ys, _, width = weight.shape
    cap = rows // blocks
    return pl.pallas_call(
        out_kernel,
        grid=(ys,),
        in_specs=[
            pl.BlockSpec((rows, units), lambda i: (0, 0)),
            pl.BlockSpec((rows, units), lambda i: (0, 0)),
            pl.BlockSpec((1, 2 * units, width), lambda i: (i, 0, 0)),
        ],
        out_specs=pl.BlockSpec((blocks, 1, cap, width), lambda i: (0, i, 0, 0)),
        out_shape=jax.ShapeDtypeStruct((blocks, ys, cap, width), jnp.bfloat16),
        compiler_params=pltpu.CompilerParams(vmem_limit_bytes=20 * 2**20),
        cost_estimate=pl.CostEstimate(
            flops=4 * rows * units * ys * width, bytes_accessed=8 * 2**20, transcendentals=0
        ),
        name="experts_out",
    )(hidden, hidden_other, weight)


def swap(value):
    return lax.ppermute(value, "core", [(0, 1), (1, 0)])


def layer_block(
    residual,
    queries,
    new_keys,
    new_values,
    key_cache,
    value_cache,
    cache_lengths,
    out_weight,
    norm_gain,
    gate_weight,
    up_weight,
    down_weight,
    routes,
    route_gates,
):
    rows, width = residual.shape
    ways = lax.axis_size("y") * lax.axis_size("core")
    share = width // ways
    planes = lax.axis_size("z")
    chips = lax.axis_size("x") * lax.axis_size("y")
    core = lax.axis_index("core")
    column = lax.axis_index("y") * CORES + core

    core_index = core.astype(jnp.int32).reshape(1)
    place = jnp.stack([core, lax.axis_index("y")]).astype(jnp.int32)
    sent, kept = attend(
        place, cache_lengths.reshape(1, -1), queries, new_keys, new_values, key_cache, value_cache, out_weight
    )
    first = kept + swap(sent).astype(jnp.float32)
    chips_y = lax.axis_size("y")
    pieces = [
        lax.ppermute(
            first[s].astype(jnp.bfloat16), "y", [(i, (i + s) % chips_y) for i in range(chips_y)]
        )
        for s in range(1, chips_y)
    ]
    gains = norm_gain.reshape(ways, share)
    first, gains, gate_weight, up_weight, down_weight = lax.optimization_barrier(
        (first, gains, gate_weight, up_weight, down_weight)
    )
    down_other = swap(down_weight)
    own_weight, other_weight = load_weights(core_index, gate_weight, up_weight)
    pieces, own_weight, other_weight = lax.optimization_barrier((pieces, own_weight, other_weight))
    start = column * share
    middle = lax.dynamic_slice_in_dim(residual, start, share, 1).astype(jnp.float32)
    middle = middle + first[0] + sum(piece.astype(jnp.float32) for piece in pieces)
    gain = lax.dynamic_slice_in_dim(norm_gain, start, share, 0)
    gained = (middle * gain).astype(jnp.bfloat16)

    named = routes[:, :, None] == jnp.arange(EXPERTS)[None, None, :]
    coef = jnp.sum(jnp.where(named, route_gates[:, :, None], 0.0), axis=1)
    taken = jnp.any(named, axis=1)
    before = jnp.arange(rows)[:, None] > jnp.arange(rows)[None, :]
    rank = jnp.dot(
        before.astype(jnp.bfloat16), taken.astype(jnp.bfloat16), preferred_element_type=jnp.float32
    )
    match = taken[:, :, None] & (rank.astype(jnp.int32)[:, :, None] == jnp.arange(CAP)[None, None, :])
    chosen = match.astype(jnp.bfloat16).reshape(rows, EXPERTS * CAP)
    blend = jnp.where(match, coef[:, :, None], 0.0).reshape(rows, EXPERTS * CAP)

    outgoing = jnp.einsum("ts,tc->sc", chosen, gained, preferred_element_type=jnp.float32)
    outgoing = outgoing.astype(jnp.bfloat16).reshape(EXPERTS, 1, CAP, share)
    outgoing = jnp.broadcast_to(outgoing, (EXPERTS, chips, CAP, share))
    own = lax.all_to_all(
        outgoing.reshape(EXPERTS * chips, CAP, share), CHIPS, split_axis=0, concat_axis=0, tiled=True
    )
    other = swap(own)

    shape = (planes * lax.axis_size("x"), lax.axis_size("y"), CAP, share)
    total, squares, out_weights = experts_first(
        core_index, own.reshape(shape), gains, own_weight, down_weight, down_other
    )
    hidden = experts_second(core_index, other.reshape(shape), gains, other_weight, total, squares)
    outs = experts_out(hidden, swap(hidden), out_weights, shape[0])
    returned = lax.all_to_all(
        outs.reshape(EXPERTS * chips, CAP, share), CHIPS, split_axis=0, concat_axis=0, tiled=True
    )
    merged = jnp.sum(
        returned.reshape(EXPERTS, chips, CAP, share).astype(jnp.float32), axis=1
    ).reshape(EXPERTS * CAP, share)
    return middle + jnp.dot(blend, merged, precision=lax.Precision.HIGHEST)


def solution(mesh):
    fine = Mesh(mesh.devices.reshape(4, 4, 4, 2), ("z", "x", "y", "core"))
    attn, expert = ("z", "x"), ("y", "core")
    every = attn + expert
    in_specs = (
        P(attn, None),
        P(attn, expert),
        P(attn, expert),
        P(attn, expert),
        P(attn, expert, None, None),
        P(attn, expert, None, None),
        P(attn),
        P(expert, None),
        P(),
        P(None, every),
        P(None, every),
        P(every, None),
        P(attn, None),
        P(attn, None),
    )
    return jax.shard_map(
        layer_block, mesh=fine, in_specs=in_specs, out_specs=P(attn, expert), check_vma=False
    )
```

time: 137 us -> 115 us (0.84)
  waiting for transfers between devices: 47.4 us -> 37.5 us
  matrix products: 10.6 us -> 1.25 us
  Pallas kernels: 15.2 us -> 19.8 us
  local copies, waits for them, and re-layouts: 4.94 us -> 0.35 us
  other arithmetic: 5.83 us -> 1.39 us
  starting transfers between devices: 10.5 us -> 11.9 us
    all_to_all x2 -> x1, waiting for transfers between devices: 40.6 us -> 32.6 us  [layer_block(): lax.all_to_all(outs.reshape(EXPERTS * chips, CAP, share), CHIPS, split_ax...]
    dot_general x4 -> x1, matrix products: 7.85 us -> 0.12 us  [layer_block(): jnp.dot(before.astype(jnp.bfloat16), taken.astype(jnp.bfloat16), preferre...]
    ppermute x0 -> x3, starting transfers between devices: none -> 5.98 us  [layer_block(): lax.ppermute(first[s].astype(jnp.bfloat16), 'y', [(i, (i + s) % chips_y)...]
    all_to_all x2 -> x1, starting transfers between devices: 10.3 us -> 5.57 us  [layer_block(): lax.all_to_all(outs.reshape(EXPERTS * chips, CAP, share), CHIPS, split_ax...]
    pallas_call x2 -> x5, Pallas kernels: 15.2 us -> 19.8 us  [the longest x1 7 us: attend(): pl.pallas_call(attend_kernel, in_specs=[scalars] + [outside] * 7, out_spe...]
    unnamed x19 -> x6, local copies, waits for them, and re-layouts: 2.61 us -> 0.01 us
    convert_element_type x4 -> x0, other arithmetic: 2.21 us -> none  [the longest x1 2.12 us: layer_block(): (kept.astype(jnp.float32) + given.astype(jnp.float32)).astype(jnp.bfloat16)]
    ppermute x2 -> x4, waiting for transfers between devices: 6.73 us -> 4.93 us  [swap(): return lax.ppermute(value, 'core', [(0, 1), (1, 0)])]
  transfers between devices with their start and end apart: 4 -> 8, of which waited for: 4 -> 4; matrix products, arithmetic and copies ran while one was open for 1% -> 1% of each run, Pallas kernels for 2% -> 5%
where the time goes in v2:
time: 115 us
  blocking collectives  42.4 us (37%)
  waiting for transfers between devices  37.5 us (33%)
  Pallas kernels  19.8 us (17%)
  starting transfers between devices  11.9 us (10%)
  other arithmetic  1.39 us (1%)
  matrix products  1.25 us (1%)
    all_to_all x1, blocking collectives, layer_block(): lax.all_to_all(outgoing.reshape(EXPERTS * chips, CAP, share), CHIPS, spli...  42.4 us
    all_to_all x1, waiting for transfers between devices, layer_block(): lax.all_to_all(outs.reshape(EXPERTS * chips, CAP, share), CHIPS, split_ax...  32.6 us
    pallas_call x1, Pallas kernels, attend(): pl.pallas_call(attend_kernel, in_specs=[scalars] + [outside] * 7, out_spe...  7 us
    ppermute x3, starting transfers between devices, layer_block(): lax.ppermute(first[s].astype(jnp.bfloat16), 'y', [(i, (i + s) % chips_y)...  5.98 us
    all_to_all x1, starting transfers between devices, layer_block(): lax.all_to_all(outs.reshape(EXPERTS * chips, CAP, share), CHIPS, split_ax...  5.57 us
    ppermute x4, waiting for transfers between devices, swap(): return lax.ppermute(value, 'core', [(0, 1), (1, 0)])  4.93 us
    pallas_call x1, Pallas kernels, experts_out(): pl.pallas_call(out_kernel, grid=(ys,), in_specs=[pl.BlockSpec((rows, unit...  4.14 us
    pallas_call x1, Pallas kernels, load_weights(): pl.pallas_call(load_kernel, in_specs=[pl.BlockSpec(memory_space=pltpu.SME...  3.83 us
  transfers between devices with their start and end apart: 8, of which 4 were waited for; matrix products, arithmetic and copies ran while one was open for 1% of the time, Pallas kernels for 5%

profile of v2, /device:TPU:0, one launch (start us, length us, event | category | flops | bytes accessed | tf_op | source)
XLA Modules:
  0.0 114.8 jit_solution(14151542625449289250)
XLA Ops:
  0.0 0.1 pad_add_fusion.place
  0.1 0.0 copy-start.1
  0.1 0.0 copy-start
  0.1 7.0 %attend.1 = (bf16[4,32,768]{2,1,0:T(8,128)(2,1)S(1)}, f32[4,32,768]{2,1,0:T(8,128)S(1)}) custom-call(s32[2]{0:T(128)S(1)} %pad_add_fusion.place, s32[1,32]{1,0:T(1,128)} %bitcast.38, bf16[32,768]{1,0:T(8,128)(2,1)} %queries.1, bf16[32,128]{1,0:T(8,128)(2,1)} %new_keys.1, bf16[32,128]{1,0:T(8,128)(2,1)} %new_values.1, bf16[32,1,320,128]{3,2,1,0:T(8,128)(2,1)} %keys.1, ...), custom_call_target="tpu_custom_call" | custom-call | flops 150994944 | bytes 15728640 | tf_op jit(solution)/shard_map/attend/pallas_call | solution.py:110
  7.1 0.1 collective-permute-start
  7.2 0.0 copy-done.1
  7.2 1.4 %collective-permute-done = bf16[4,32,768]{2,1,0:T(8,128)(2,1)S(1)} collective-permute-done((bf16[4,32,768]{2,1,0:T(8,128)(2,1)S(1)}, bf16[4,32,768]{2,1,0:T(8,128)(2,1)S(1)}, u32[]{:S(2)}, u32[]{:S(2)}) %collective-permute-start) | collective-permute-done | bytes 196640 | tf_op jit(solution)/shard_map/ppermute | solution.py:295
  8.6 0.1 fusion.13
  8.7 1.7 %collective-permute-start.1 = (bf16[32,768]{1,0:T(8,128)(2,1)S(1)}, bf16[32,768]{1,0:T(8,128)(2,1)S(1)}, u32[]{:S(2)}, u32[]{:S(2)}) collective-permute-start(bf16[32,768]{1,0:T(8,128)(2,1)S(1)} %get-tuple-element.43), channel_id=1, source_target_pairs={{0,2},{2,4},{4,6},{6,0},{1,3},{3,5},{5,7},{7,1},{8,10},{10,12},{12... | collective-permute-start | bytes 147464 | tf_op jit(solution)/shard_map/ppermute | solution.py:330
  10.4 2.9 %collective-permute-start.2 = (bf16[32,768]{1,0:T(8,128)(2,1)S(1)}, bf16[32,768]{1,0:T(8,128)(2,1)S(1)}, u32[]{:S(2)}, u32[]{:S(2)}) collective-permute-start(bf16[32,768]{1,0:T(8,128)(2,1)S(1)} %get-tuple-element.42), channel_id=1, source_target_pairs={{0,4},{2,6},{4,0},{6,2},{1,5},{3,7},{5,1},{7,3},{8,12},{10,14},{12... | collective-permute-start | bytes 147464 | tf_op jit(solution)/shard_map/ppermute | solution.py:330
  13.3 1.3 %collective-permute-start.3 = (bf16[32,768]{1,0:T(8,128)(2,1)S(1)}, bf16[32,768]{1,0:T(8,128)(2,1)S(1)}, u32[]{:S(2)}, u32[]{:S(2)}) collective-permute-start(bf16[32,768]{1,0:T(8,128)(2,1)S(1)} %get-tuple-element.41), channel_id=1, source_target_pairs={{0,6},{2,0},{4,2},{6,4},{1,7},{3,1},{5,3},{7,5},{8,14},{10,8},{12,... | collective-permute-start | bytes 147464 | tf_op jit(solution)/shard_map/ppermute | solution.py:330
  14.7 0.1 convolution_convert_fusion.1
  14.8 0.0 copy-done
  14.8 0.1 dynamic_slice.7
  14.9 0.1 eq.45
  15.0 0.1 fusion.6
  15.1 0.1 collective-permute-start.5
  15.2 3.8 %load_weights.1 = (bf16[4,768,768]{2,1,0:T(8,128)(2,1)S(1)}, bf16[4,768,768]{2,1,0:T(8,128)(2,1)S(1)}) custom-call(s32[1]{0:T(128)} %bitcast.core, bf16[6144,384]{1,0:T(8,128)(2,1)} %gate, bf16[6144,384]{1,0:T(8,128)(2,1)} %up), custom_call_target="tpu_custom_call" | custom-call | bytes 19922944 | tf_op jit(solution)/shard_map/load_weights/pallas_call | solution.py:159
  19.0 0.0 collective-permute-done.1
  19.0 0.0 collective-permute-done.2
  19.0 0.0 collective-permute-done.3
  19.0 0.8 fusion.1
  19.9 0.2 convolution_convert_fusion
  20.1 0.2 broadcast_in_dim.46
  20.2 42.4 %all_to_all.10 = bf16[64,24,768]{2,1,0:T(8,128)(2,1)S(1)} all-to-all(bf16[64,24,768]{2,1,0:T(8,128)(2,1)S(1)} %bitcast.36), channel_id=1, replica_groups=mesh['z'=4,'x'=4,'y'=4,'core'=2] {'z','x','y'}, dimensions={0} | all-to-all | bytes 4718592 | tf_op jit(solution)/shard_map/all_to_all | solution.py:362
  62.6 0.0 collective-permute-start.4
  62.6 0.0 collective-permute-done.5.down_other
  62.6 2.5 %experts_first.1 = (f32[384,768]{1,0:T(8,128)S(1)}, f32[384,128]{1,0:T(8,128)S(1)}, bf16[4,768,768]{2,1,0:T(8,128)(2,1)S(1)}) custom-call(s32[1]{0:T(128)} %bitcast.core, bf16[16,4,24,768]{3,2,1,0:T(8,128)(2,1)S(1)} %bitcast.34, f32[8,768]{1,0:T(8,128)S(1)} %reshape.40.gain, bf16[4,768,768]{2,1,0:T(8,128)(2,1)S(1)} %get-tuple-element.34.weight, ...), custom_call_target="tpu_custom_call" | custom-call | flops 1811939328 | bytes 12582912 | tf_op jit(solution)/shard_map/experts_first/pallas_call | solution.py:237
  65.1 2.1 %collective-permute-done.4 = bf16[64,24,768]{2,1,0:T(8,128)(2,1)S(1)} collective-permute-done((bf16[64,24,768]{2,1,0:T(8,128)(2,1)S(1)}, bf16[64,24,768]{2,1,0:T(8,128)(2,1)S(1)}, u32[]{:S(2)}, u32[]{:S(2)}) %collective-permute-start.4) | collective-permute-done | bytes 2359328 | tf_op jit(solution)/shard_map/ppermute | solution.py:295
  67.1 2.4 %experts_second.1.hidden = bf16[384,384]{1,0:T(8,128)(2,1)S(1)} custom-call(s32[1]{0:T(128)} %bitcast.core, bf16[16,4,24,768]{3,2,1,0:T(8,128)(2,1)S(1)} %bitcast.35, f32[8,768]{1,0:T(8,128)S(1)} %reshape.40.gain, bf16[4,768,768]{2,1,0:T(8,128)(2,1)S(1)} %get-tuple-element.33.weight, f32[384,768]{1,0:T(8,128)S(1)} %get-tuple-element.36.total_ref, ...), custom_call_target="tpu_custom_call" | custom-call | flops 1811939328 | bytes 12582912 | tf_op jit(solution)/shard_map/experts_second/pallas_call | solution.py:259
  69.5 0.2 collective-permute-start.6
  69.7 1.5 %collective-permute-done.6.hidden_other = bf16[384,384]{1,0:T(8,128)(2,1)S(1)} collective-permute-done((bf16[384,384]{1,0:T(8,128)(2,1)S(1)}, bf16[384,384]{1,0:T(8,128)(2,1)S(1)}, u32[]{:S(2)}, u32[]{:S(2)}) %collective-permute-start.6) | collective-permute-done | bytes 294944 | tf_op jit(solution)/shard_map/ppermute | solution.py:295
  71.2 0.0 copy-start.2
  71.2 4.1 %experts_out.1 = bf16[16,4,24,768]{3,2,1,0:T(8,128)(2,1)} custom-call(bf16[384,384]{1,0:T(8,128)(2,1)S(1)} %experts_second.1.hidden, bf16[384,384]{1,0:T(8,128)(2,1)S(1)} %collective-permute-done.6.hidden_other, bf16[4,768,768]{2,1,0:T(8,128)(2,1)S(1)} %get-tuple-element.38.weight), custom_call_target="tpu_custom_call" | custom-call | flops 1811939328 | bytes 8388608 | tf_op jit(solution)/shard_map/experts_out/pallas_call | solution.py:276
  75.3 5.6 %all-to-all-start.1 = ((bf16[64,24,768]{2,1,0:T(8,128)(2,1)}), bf16[64,24,768]{2,1,0:T(8,128)(2,1)S(1)}, u32[]{:S(2)}, u32[]{:S(2)}) async-start(bf16[64,24,768]{2,1,0:T(8,128)(2,1)} %bitcast.13), calls=%async_computation.1 | async-start | bytes 4718592 | tf_op jit(solution)/shard_map/all_to_all | solution.py:373
  80.9 0.0 copy-done.2
  80.9 32.6 %all-to-all-done.1 = bf16[64,24,768]{2,1,0:T(8,128)(2,1)S(1)} async-done(((bf16[64,24,768]{2,1,0:T(8,128)(2,1)}), bf16[64,24,768]{2,1,0:T(8,128)(2,1)S(1)}, u32[]{:S(2)}, u32[]{:S(2)}) %all-to-all-start.1) | async-done | bytes 2359328 | tf_op jit(solution)/shard_map/all_to_all | solution.py:373
  113.5 0.3 convert_reduce_fusion
  113.8 1.0 fusion
  (5 shorter events, 0.1 us)
Async XLA Ops:
  0.1 7.1 %copy-start.1 = (s32[32,2]{0,1:T(2,128)S(1)}, s32[32,2]{0,1:T(2,128)}, u32[]{:S(2)}) copy-start(s32[32,2]{0,1:T(2,128)} %param.26) | copy-start | bytes 772
  0.1 14.7 %copy-start = (f32[6144]{0:T(1024)S(1)}, f32[6144]{0:T(1024)}, u32[]{:S(2)}) copy-start(f32[6144]{0:T(1024)} %param.22) | copy-start | bytes 73732
  7.1 1.5 %collective-permute-start = (bf16[4,32,768]{2,1,0:T(8,128)(2,1)S(1)}, bf16[4,32,768]{2,1,0:T(8,128)(2,1)S(1)}, u32[]{:S(2)}, u32[]{:S(2)}) collective-permute-start(bf16[4,32,768]{2,1,0:T(8,128)(2,1)S(1)} %get-tuple-element.23), channel_id=1, source_target_pairs={{0,1},{1,0},{2,3},{3,2},{4,5},{5,4},{6,7},{7,6},{8,9},{9,8},{10,11... | collective-permute-start | bytes 589832 | tf_op jit(solution)/shard_map/ppermute | solution.py:295
  8.7 10.3 %collective-permute-start.1 = (bf16[32,768]{1,0:T(8,128)(2,1)S(1)}, bf16[32,768]{1,0:T(8,128)(2,1)S(1)}, u32[]{:S(2)}, u32[]{:S(2)}) collective-permute-start(bf16[32,768]{1,0:T(8,128)(2,1)S(1)} %get-tuple-element.43), channel_id=1, source_target_pairs={{0,2},{2,4},{4,6},{6,0},{1,3},{3,5},{5,7},{7,1},{8,10},{10,12},{12... | collective-permute-start | bytes 147464 | tf_op jit(solution)/shard_map/ppermute | solution.py:330
  10.4 8.6 %collective-permute-start.2 = (bf16[32,768]{1,0:T(8,128)(2,1)S(1)}, bf16[32,768]{1,0:T(8,128)(2,1)S(1)}, u32[]{:S(2)}, u32[]{:S(2)}) collective-permute-start(bf16[32,768]{1,0:T(8,128)(2,1)S(1)} %get-tuple-element.42), channel_id=1, source_target_pairs={{0,4},{2,6},{4,0},{6,2},{1,5},{3,7},{5,1},{7,3},{8,12},{10,14},{12... | collective-permute-start | bytes 147464 | tf_op jit(solution)/shard_map/ppermute | solution.py:330
  13.3 5.7 %collective-permute-start.3 = (bf16[32,768]{1,0:T(8,128)(2,1)S(1)}, bf16[32,768]{1,0:T(8,128)(2,1)S(1)}, u32[]{:S(2)}, u32[]{:S(2)}) collective-permute-start(bf16[32,768]{1,0:T(8,128)(2,1)S(1)} %get-tuple-element.41), channel_id=1, source_target_pairs={{0,6},{2,0},{4,2},{6,4},{1,7},{3,1},{5,3},{7,5},{8,14},{10,8},{12,... | collective-permute-start | bytes 147464 | tf_op jit(solution)/shard_map/ppermute | solution.py:330
  15.1 47.5 %collective-permute-start.5 = (bf16[384,6144]{1,0:T(8,128)(2,1)}, bf16[384,6144]{1,0:T(8,128)(2,1)S(1)}, u32[]{:S(2)}, u32[]{:S(2)}) collective-permute-start(bf16[384,6144]{1,0:T(8,128)(2,1)} %down), channel_id=1, source_target_pairs={{0,1},{1,0},{2,3},{3,2},{4,5},{5,4},{6,7},{7,6},{8,9},{9,8},{10,11... | collective-permute-start | bytes 14155784 | tf_op jit(solution)/shard_map/ppermute | solution.py:295
  62.6 4.5 %collective-permute-start.4 = (bf16[64,24,768]{2,1,0:T(8,128)(2,1)S(1)}, bf16[64,24,768]{2,1,0:T(8,128)(2,1)S(1)}, u32[]{:S(2)}, u32[]{:S(2)}) collective-permute-start(bf16[64,24,768]{2,1,0:T(8,128)(2,1)S(1)} %all_to_all.10), channel_id=1, source_target_pairs={{0,1},{1,0},{2,3},{3,2},{4,5},{5,4},{6,7},{7,6},{8,9},{9,8},{10,11... | collective-permute-start | bytes 7077896 | tf_op jit(solution)/shard_map/ppermute | solution.py:295
  69.5 1.7 %collective-permute-start.6 = (bf16[384,384]{1,0:T(8,128)(2,1)S(1)}, bf16[384,384]{1,0:T(8,128)(2,1)S(1)}, u32[]{:S(2)}, u32[]{:S(2)}) collective-permute-start(bf16[384,384]{1,0:T(8,128)(2,1)S(1)} %experts_second.1.hidden), channel_id=1, source_target_pairs={{0,1},{1,0},{2,3},{3,2},{4,5},{5,4},{6,7},{7,6},{8,9},{9,8},{10,11... | collective-permute-start | bytes 884744 | tf_op jit(solution)/shard_map/ppermute | solution.py:295
  71.2 9.7 %copy-start.2 = (f32[32,2]{0,1:T(2,128)S(1)}, f32[32,2]{0,1:T(2,128)}, u32[]{:S(2)}) copy-start(f32[32,2]{0,1:T(2,128)} %param.27) | copy-start | bytes 772
  75.3 38.2 %all-to-all-start.1 = ((bf16[64,24,768]{2,1,0:T(8,128)(2,1)}), bf16[64,24,768]{2,1,0:T(8,128)(2,1)S(1)}, u32[]{:S(2)}, u32[]{:S(2)}) async-start(bf16[64,24,768]{2,1,0:T(8,128)(2,1)} %bitcast.13), calls=%async_computation.1 | async-start | bytes 4718592 | tf_op jit(solution)/shard_map/all_to_all | solution.py:373

commit v3 on v2

--- a/solution.py
+++ b/solution.py
@@ -13,8 +13,25 @@
 CORES = 2
 EPSILON = 1e-05
 
-CHIPS = ("z", "x", "y")
-GROUP = ("y", "core")
+EVERY = ("z", "x", "y", "core")
+FLIP = 2
+CHIP_ORDERS = [
+    [
+        (((z ^ (FLIP * c)) * 4 + (x ^ (FLIP * c))) * 4 + (y ^ (FLIP * c))) * CORES + c
+        for y in range(4)
+        for z in range(4)
+        for x in range(4)
+    ]
+    for c in range(CORES)
+]
+
+
+def exchange(blocks):
+    flat = blocks.reshape(64, *blocks.shape[3:])
+    flat = lax.all_to_all(
+        flat, EVERY, split_axis=0, concat_axis=0, axis_index_groups=CHIP_ORDERS, tiled=True
+    )
+    return flat.reshape(blocks.shape)
 
 
 PART = 8
@@ -143,9 +160,8 @@
     return [pltpu.make_async_copy(s, t, sems.at[i]) for i, (s, t) in enumerate(copies)]
 
 
-def load_kernel(core, gate, up, own_weight, other_weight, sems):
-    copies = gate_up_copies(core[0], gate, up, own_weight, sems.at[0])
-    copies += gate_up_copies(1 - core[0], gate, up, other_weight, sems.at[1])
+def load_kernel(core, gate, up, own_weight, sems):
+    copies = gate_up_copies(core[0], gate, up, own_weight, sems)
     for copy in copies:
         copy.start()
     for copy in copies:
@@ -159,11 +175,11 @@
     return pl.pallas_call(
         load_kernel,
         in_specs=[pl.BlockSpec(memory_space=pltpu.SMEM)] + [outside] * 2,
-        out_specs=[inside] * 2,
-        out_shape=[jax.ShapeDtypeStruct((ys, width, 2 * units), jnp.bfloat16)] * 2,
-        scratch_shapes=[pltpu.SemaphoreType.DMA((2, 2 * ys))],
+        out_specs=inside,
+        out_shape=jax.ShapeDtypeStruct((ys, width, 2 * units), jnp.bfloat16),
+        scratch_shapes=[pltpu.SemaphoreType.DMA((2 * ys,))],
         compiler_params=pltpu.CompilerParams(vmem_limit_bytes=16 * 2**20),
-        cost_estimate=pl.CostEstimate(flops=0, bytes_accessed=19 * 2**20, transcendentals=0),
+        cost_estimate=pl.CostEstimate(flops=0, bytes_accessed=9 * 2**20, transcendentals=0),
         name="load_weights",
     )(core, *in_hbm(gate, up))
 
@@ -179,10 +195,16 @@
 
 
 def add_products(side, source, gain, weight, total, squares):
-    blocks, ys, cap, width = source.shape
-    rows = blocks * cap
+    ys, zs, xs, cap, width = source.shape
+    rows = zs * xs * cap
+    flip = FLIP * side
     for y in range(ys):
-        wide = source[:, y].astype(jnp.float32).reshape(rows, width)
+        parts = [
+            source[y ^ flip, z ^ flip, pl.ds(x ^ flip, FLIP)]
+            for z in range(zs)
+            for x in range(0, xs, FLIP)
+        ]
+        wide = jnp.concatenate(parts, axis=0).astype(jnp.float32).reshape(rows, width)
         inverse = 1.0 / gain[pl.ds(2 * y + side, 1), :]
         parts = wide * wide * (inverse * inverse)
         step = parts[:, 0:128]
@@ -197,9 +219,11 @@
 
 
 def first_kernel(
-    core, own, gain, weight, down, down_other, total_ref, squares_ref, out_weight, sems
+    core, own, gain, weight, gate, up, down, down_other,
+    total_ref, squares_ref, other_weight, out_weight, sems,
 ):
-    copies = down_copies(core[0], down, down_other, out_weight, sems)
+    copies = gate_up_copies(1 - core[0], gate, up, other_weight, sems.at[0])
+    copies += down_copies(core[0], down, down_other, out_weight, sems.at[1])
     for copy in copies:
         copy.start()
     total, squares = add_products(core[0], own, gain, weight, None, None)
@@ -210,7 +234,7 @@
 
 
 def second_kernel(core, other, gain, weight, total_ref, squares_ref, hidden_ref):
-    ys, width = other.shape[1], other.shape[3]
+    ys, width = other.shape[0], other.shape[4]
     total, squares = add_products(
         1 - core[0], other, gain, weight, total_ref[...], squares_ref[...]
     )
@@ -221,35 +245,50 @@
     hidden_ref[...] = (gate_sum / (1.0 + jnp.exp(-gate_sum)) * up_sum).astype(jnp.bfloat16)
 
 
-def out_kernel(hidden, hidden_other, weight, out_ref):
-    blocks, _, cap, width = out_ref.shape
-    units = hidden.shape[1]
-    out = jnp.dot(hidden[...], weight[0, :units], preferred_element_type=jnp.float32)
-    out += jnp.dot(hidden_other[...], weight[0, units:], preferred_element_type=jnp.float32)
-    out_ref[...] = out.reshape(blocks, 1, cap, width).astype(out_ref.dtype)
-
-
-def experts_first(core, own, gain, weight, down, down_other):
-    blocks, ys, cap, width = own.shape
-    rows, units = blocks * cap, down.shape[0]
+def out_kernel(core, hidden, hidden_other, weight, out_ref, buf, sems):
+    ys, zs, xs, cap, width = out_ref.shape
+    flip = FLIP * core[0]
+    both = jnp.concatenate([hidden[...], hidden_other[...]], axis=1)
+    copies = []
+    for y in range(ys):
+        out = jnp.dot(both, weight[y], preferred_element_type=jnp.float32)
+        buf[y] = out.reshape(zs, xs, cap, width).astype(buf.dtype)
+        for z in range(zs):
+            for x in range(0, xs, FLIP):
+                copies.append(
+                    pltpu.make_async_copy(
+                        buf.at[y, z, pl.ds(x, FLIP)],
+                        out_ref.at[y ^ flip, z ^ flip, pl.ds(x ^ flip, FLIP)],
+                        sems.at[len(copies)],
+                    )
+                )
+                copies[-1].start()
+    for copy in copies:
+        copy.wait()
+
+
+def experts_first(core, own, gain, weight, gate, up, down, down_other):
+    ys, zs, xs, cap, width = own.shape
+    rows, units = zs * xs * cap, down.shape[0]
     inside = pl.BlockSpec(memory_space=pltpu.VMEM)
     outside = pl.BlockSpec(memory_space=pltpu.HBM)
     return pl.pallas_call(
         first_kernel,
-        in_specs=[pl.BlockSpec(memory_space=pltpu.SMEM)] + [inside] * 3 + [outside, pl.BlockSpec(memory_space=pl.ANY)],
-        out_specs=[inside] * 3,
+        in_specs=[pl.BlockSpec(memory_space=pltpu.SMEM)] + [inside] * 3 + [outside] * 3 + [pl.BlockSpec(memory_space=pl.ANY)],
+        out_specs=[inside] * 4,
         out_shape=[
             jax.ShapeDtypeStruct((rows, 2 * units), jnp.float32),
             jax.ShapeDtypeStruct((rows, 128), jnp.float32),
+            jax.ShapeDtypeStruct((ys, width, 2 * units), jnp.bfloat16),
             jax.ShapeDtypeStruct((ys, 2 * units, width), jnp.bfloat16),
         ],
-        scratch_shapes=[pltpu.SemaphoreType.DMA((2 * ys,))],
+        scratch_shapes=[pltpu.SemaphoreType.DMA((2, 2 * ys))],
         compiler_params=pltpu.CompilerParams(vmem_limit_bytes=16 * 2**20),
         cost_estimate=pl.CostEstimate(
             flops=4 * rows * units * ys * width, bytes_accessed=12 * 2**20, transcendentals=0
         ),
         name="experts_first",
-    )(core, own, gain, weight, *in_hbm(down), down_other)
+    )(core, own, gain, weight, *in_hbm(gate, up, down), down_other)
 
 
 def experts_second(core, other, gain, weight, total, squares):
@@ -269,26 +308,25 @@
     )(core, pltpu.with_memory_space_constraint(other, pltpu.VMEM), gain, weight, total, squares)
 
 
-def experts_out(hidden, hidden_other, weight, blocks):
+def experts_out(core, hidden, hidden_other, weight, shape):
     rows, units = hidden.shape
-    ys, _, width = weight.shape
-    cap = rows // blocks
+    ys, zs, xs, cap, width = shape
+    inside = pl.BlockSpec(memory_space=pltpu.VMEM)
     return pl.pallas_call(
         out_kernel,
-        grid=(ys,),
-        in_specs=[
-            pl.BlockSpec((rows, units), lambda i: (0, 0)),
-            pl.BlockSpec((rows, units), lambda i: (0, 0)),
-            pl.BlockSpec((1, 2 * units, width), lambda i: (i, 0, 0)),
+        in_specs=[pl.BlockSpec(memory_space=pltpu.SMEM)] + [inside] * 3,
+        out_specs=pl.BlockSpec(memory_space=pltpu.HBM),
+        out_shape=jax.ShapeDtypeStruct(shape, jnp.bfloat16),
+        scratch_shapes=[
+            pltpu.VMEM((ys, zs, xs, cap, width), jnp.bfloat16),
+            pltpu.SemaphoreType.DMA((ys * zs * xs // FLIP,)),
         ],
-        out_specs=pl.BlockSpec((blocks, 1, cap, width), lambda i: (0, i, 0, 0)),
-        out_shape=jax.ShapeDtypeStruct((blocks, ys, cap, width), jnp.bfloat16),
         compiler_params=pltpu.CompilerParams(vmem_limit_bytes=20 * 2**20),
         cost_estimate=pl.CostEstimate(
             flops=4 * rows * units * ys * width, bytes_accessed=8 * 2**20, transcendentals=0
         ),
         name="experts_out",
-    )(hidden, hidden_other, weight)
+    )(core, hidden, hidden_other, weight)
 
 
 def swap(value):
@@ -314,8 +352,7 @@
     rows, width = residual.shape
     ways = lax.axis_size("y") * lax.axis_size("core")
     share = width // ways
-    planes = lax.axis_size("z")
-    chips = lax.axis_size("x") * lax.axis_size("y")
+    shape = (lax.axis_size("y"), lax.axis_size("z"), lax.axis_size("x"), CAP, share)
     core = lax.axis_index("core")
     column = lax.axis_index("y") * CORES + core
 
@@ -337,15 +374,16 @@
         (first, gains, gate_weight, up_weight, down_weight)
     )
     down_other = swap(down_weight)
-    own_weight, other_weight = load_weights(core_index, gate_weight, up_weight)
-    pieces, own_weight, other_weight = lax.optimization_barrier((pieces, own_weight, other_weight))
+    own_weight = load_weights(core_index, gate_weight, up_weight)
+    pieces, own_weight = lax.optimization_barrier((pieces, own_weight))
     start = column * share
     middle = lax.dynamic_slice_in_dim(residual, start, share, 1).astype(jnp.float32)
     middle = middle + first[0] + sum(piece.astype(jnp.float32) for piece in pieces)
     gain = lax.dynamic_slice_in_dim(norm_gain, start, share, 0)
     gained = (middle * gain).astype(jnp.bfloat16)
 
-    named = routes[:, :, None] == jnp.arange(EXPERTS)[None, None, :]
+    order = jnp.arange(EXPERTS) ^ (FLIP * core)
+    named = routes[:, :, None] == order[None, None, :]
     coef = jnp.sum(jnp.where(named, route_gates[:, :, None], 0.0), axis=1)
     taken = jnp.any(named, axis=1)
     before = jnp.arange(rows)[:, None] > jnp.arange(rows)[None, :]
@@ -357,25 +395,17 @@
     blend = jnp.where(match, coef[:, :, None], 0.0).reshape(rows, EXPERTS * CAP)
 
     outgoing = jnp.einsum("ts,tc->sc", chosen, gained, preferred_element_type=jnp.float32)
-    outgoing = outgoing.astype(jnp.bfloat16).reshape(EXPERTS, 1, CAP, share)
-    outgoing = jnp.broadcast_to(outgoing, (EXPERTS, chips, CAP, share))
-    own = lax.all_to_all(
-        outgoing.reshape(EXPERTS * chips, CAP, share), CHIPS, split_axis=0, concat_axis=0, tiled=True
-    )
+    outgoing = outgoing.astype(jnp.bfloat16).reshape(1, EXPERTS, 1, CAP, share)
+    own = exchange(jnp.broadcast_to(outgoing, shape))
     other = swap(own)
 
-    shape = (planes * lax.axis_size("x"), lax.axis_size("y"), CAP, share)
-    total, squares, out_weights = experts_first(
-        core_index, own.reshape(shape), gains, own_weight, down_weight, down_other
-    )
-    hidden = experts_second(core_index, other.reshape(shape), gains, other_weight, total, squares)
-    outs = experts_out(hidden, swap(hidden), out_weights, shape[0])
-    returned = lax.all_to_all(
-        outs.reshape(EXPERTS * chips, CAP, share), CHIPS, split_axis=0, concat_axis=0, tiled=True
-    )
-    merged = jnp.sum(
-        returned.reshape(EXPERTS, chips, CAP, share).astype(jnp.float32), axis=1
-    ).reshape(EXPERTS * CAP, share)
+    total, squares, other_weight, out_weights = experts_first(
+        core_index, own, gains, own_weight, gate_weight, up_weight, down_weight, down_other
+    )
+    hidden = experts_second(core_index, other, gains, other_weight, total, squares)
+    outs = experts_out(core_index, hidden, swap(hidden), out_weights, shape)
+    returned = exchange(outs)
+    merged = jnp.sum(returned.astype(jnp.float32), axis=(0, 2)).reshape(EXPERTS * CAP, share)
     return middle + jnp.dot(blend, merged, precision=lax.Precision.HIGHEST)
 
 

time: 115 us -> 110 us (0.957)
  waiting for transfers between devices: 37.5 us -> 33.7 us
  starting transfers between devices: 11.9 us -> 14.9 us
  blocking collectives: 42.4 us -> 39.6 us
  Pallas kernels: 19.8 us -> 18.1 us
    all_to_all x1, waiting for transfers between devices: 32.6 us -> 29.6 us  [exchange(): lax.all_to_all(flat, EVERY, split_axis=0, concat_axis=0, axis_index_group...]
    all_to_all x1, starting transfers between devices: 5.57 us -> 8.32 us  [exchange(): lax.all_to_all(flat, EVERY, split_axis=0, concat_axis=0, axis_index_group...]
    all_to_all x1, blocking collectives: 42.4 us -> 39.6 us  [exchange(): lax.all_to_all(flat, EVERY, split_axis=0, concat_axis=0, axis_index_group...]
    pallas_call x1, Pallas kernels: 3.83 us -> 2.39 us  [load_weights(): pl.pallas_call(load_kernel, in_specs=[pl.BlockSpec(memory_space=pltpu.SME...]
  transfers between devices with their start and end apart: 8 -> 8, of which waited for: 4 -> 4; matrix products, arithmetic and copies ran while one was open for 1% -> 2% of each run, Pallas kernels for 5% -> 5%
where the time goes in v3:
time: 110 us
  blocking collectives  39.6 us (36%)
  waiting for transfers between devices  33.7 us (31%)
  Pallas kernels  18.1 us (16%)
  starting transfers between devices  14.9 us (14%)
  other arithmetic  1.52 us (1%)
  matrix products  1.26 us (1%)
    all_to_all x1, blocking collectives, exchange(): lax.all_to_all(flat, EVERY, split_axis=0, concat_axis=0, axis_index_group...  39.6 us
    all_to_all x1, waiting for transfers between devices, exchange(): lax.all_to_all(flat, EVERY, split_axis=0, concat_axis=0, axis_index_group...  29.6 us
    all_to_all x1, starting transfers between devices, exchange(): lax.all_to_all(flat, EVERY, split_axis=0, concat_axis=0, axis_index_group...  8.32 us
    pallas_call x1, Pallas kernels, attend(): pl.pallas_call(attend_kernel, in_specs=[scalars] + [outside] * 7, out_spe...  7.01 us
    ppermute x3, starting transfers between devices, layer_block(): lax.ppermute(first[s].astype(jnp.bfloat16), 'y', [(i, (i + s) % chips_y)...  5.98 us
    ppermute x4, waiting for transfers between devices, swap(): return lax.ppermute(value, 'core', [(0, 1), (1, 0)])  4.07 us
    pallas_call x1, Pallas kernels, experts_first(): pl.pallas_call(first_kernel, in_specs=[pl.BlockSpec(memory_space=pltpu.SM...  3.2 us
    pallas_call x1, Pallas kernels, experts_out(): pl.pallas_call(out_kernel, in_specs=[pl.BlockSpec(memory_space=pltpu.SMEM...  3.19 us
  transfers between devices with their start and end apart: 8, of which 4 were waited for; matrix products, arithmetic and copies ran while one was open for 2% of the time, Pallas kernels for 5%

profile of v3, /device:TPU:0, one launch (start us, length us, event | category | flops | bytes accessed | tf_op | source)
XLA Modules:
  0.0 109.6 jit_solution(15148711246784991189)
XLA Ops:
  0.0 0.1 pad_add_fusion.place
  0.1 0.0 copy-start.1
  0.1 0.0 copy-start
  0.1 7.0 %attend.1 = (bf16[4,32,768]{2,1,0:T(8,128)(2,1)S(1)}, f32[4,32,768]{2,1,0:T(8,128)S(1)}) custom-call(s32[2]{0:T(128)S(1)} %pad_add_fusion.place, s32[1,32]{1,0:T(1,128)} %bitcast.37, bf16[32,768]{1,0:T(8,128)(2,1)} %queries.1, bf16[32,128]{1,0:T(8,128)(2,1)} %new_keys.1, bf16[32,128]{1,0:T(8,128)(2,1)} %new_values.1, bf16[32,1,320,128]{3,2,1,0:T(8,128)(2,1)} %keys.1, ...), custom_call_target="tpu_custom_call" | custom-call | flops 150994944 | bytes 15728640 | tf_op jit(solution)/shard_map/attend/pallas_call | solution.py:127
  7.1 0.1 collective-permute-start
  7.2 0.0 copy-done.1
  7.2 0.1 compare_reduce_fusion
  7.3 1.3 %collective-permute-done = bf16[4,32,768]{2,1,0:T(8,128)(2,1)S(1)} collective-permute-done((bf16[4,32,768]{2,1,0:T(8,128)(2,1)S(1)}, bf16[4,32,768]{2,1,0:T(8,128)(2,1)S(1)}, u32[]{:S(2)}, u32[]{:S(2)}) %collective-permute-start) | collective-permute-done | bytes 196640 | tf_op jit(solution)/shard_map/ppermute | solution.py:333
  8.7 1.7 %collective-permute-start.1 = (bf16[32,768]{1,0:T(8,128)(2,1)S(1)}, bf16[32,768]{1,0:T(8,128)(2,1)S(1)}, u32[]{:S(2)}, u32[]{:S(2)}) collective-permute-start(bf16[32,768]{1,0:T(8,128)(2,1)S(1)} %get-tuple-element.39), channel_id=1, source_target_pairs={{0,2},{2,4},{4,6},{6,0},{1,3},{3,5},{5,7},{7,1},{8,10},{10,12},{12... | collective-permute-start | bytes 147464 | tf_op jit(solution)/shard_map/ppermute | solution.py:367
  10.4 2.9 %collective-permute-start.2 = (bf16[32,768]{1,0:T(8,128)(2,1)S(1)}, bf16[32,768]{1,0:T(8,128)(2,1)S(1)}, u32[]{:S(2)}, u32[]{:S(2)}) collective-permute-start(bf16[32,768]{1,0:T(8,128)(2,1)S(1)} %get-tuple-element.38), channel_id=1, source_target_pairs={{0,4},{2,6},{4,0},{6,2},{1,5},{3,7},{5,1},{7,3},{8,12},{10,14},{12... | collective-permute-start | bytes 147464 | tf_op jit(solution)/shard_map/ppermute | solution.py:367
  13.3 1.3 %collective-permute-start.3 = (bf16[32,768]{1,0:T(8,128)(2,1)S(1)}, bf16[32,768]{1,0:T(8,128)(2,1)S(1)}, u32[]{:S(2)}, u32[]{:S(2)}) collective-permute-start(bf16[32,768]{1,0:T(8,128)(2,1)S(1)} %get-tuple-element.37), channel_id=1, source_target_pairs={{0,6},{2,0},{4,2},{6,4},{1,7},{3,1},{5,3},{7,5},{8,14},{10,8},{12,... | collective-permute-start | bytes 147464 | tf_op jit(solution)/shard_map/ppermute | solution.py:367
  14.7 0.1 convolution_convert_fusion.1
  14.8 0.0 copy-done
  14.8 0.1 dynamic_slice.7
  14.9 0.1 eq.45
  15.0 0.1 fusion.6
  15.1 0.1 collective-permute-start.5
  15.2 2.4 %load_weights.1.weight = bf16[4,768,768]{2,1,0:T(8,128)(2,1)S(1)} custom-call(s32[1]{0:T(128)} %bitcast.core, bf16[6144,384]{1,0:T(8,128)(2,1)} %gate.1, bf16[6144,384]{1,0:T(8,128)(2,1)} %up.1), custom_call_target="tpu_custom_call" | custom-call | bytes 9437184 | tf_op jit(solution)/shard_map/load_weights/pallas_call | solution.py:175
  17.6 0.0 collective-permute-done.1
  17.6 0.0 collective-permute-done.2
  17.6 0.0 collective-permute-done.3
  17.6 0.8 fusion.1
  18.4 0.2 convolution_convert_fusion
  18.6 0.2 broadcast_in_dim.46
  18.8 39.6 %all_to_all.10 = bf16[64,24,768]{2,1,0:T(8,128)(2,1)S(1)} all-to-all(bf16[64,24,768]{2,1,0:T(8,128)(2,1)S(1)} %bitcast.35), channel_id=1, replica_groups={{0,8,16,24,32,40,48,56,64,72,80,88,96,104,112,120,2,10,18,26,34,42,50,5..., dimensions={0} | all-to-all | bytes 4718592 | tf_op jit(solution)/shard_map/all_to_all | solution.py:31
  58.4 0.0 collective-permute-start.4
  58.4 0.0 collective-permute-done.5.down_other
  58.4 3.2 %experts_first.1 = (f32[384,768]{1,0:T(8,128)S(1)}, f32[384,128]{1,0:T(8,128)S(1)}, bf16[4,768,768]{2,1,0:T(8,128)(2,1)S(1)}, bf16[4,768,768]{2,1,0:T(8,128)(2,1)S(1)}) custom-call(s32[1]{0:T(128)} %bitcast.core, bf16[4,4,4,24,768]{4,3,2,1,0:T(8,128)(2,1)S(1)} %bitcast.33, f32[8,768]{1,0:T(8,128)S(1)} %reshape.41.gain, ...), custom_call_target="tpu_custom_call" | custom-call | flops 1811939328 | bytes 12582912 | tf_op jit(solution)/shard_map/experts_first/pallas_call | solution.py:275
  61.6 1.3 %collective-permute-done.4.other = bf16[4,4,4,24,768]{4,3,2,1,0:T(8,128)(2,1)S(1)} collective-permute-done((bf16[4,4,4,24,768]{4,3,2,1,0:T(8,128)(2,1)S(1)}, bf16[4,4,4,24,768]{4,3,2,1,0:T(8,128)(2,1)S(1)}, u32[]{:S(2)}, u32[]{:S(2)}) %collective-permute-start.4) | collective-permute-done | bytes 2359328 | tf_op jit(solution)/shard_map/ppermute | solution.py:333
  62.9 2.4 %experts_second.1.hidden = bf16[384,384]{1,0:T(8,128)(2,1)S(1)} custom-call(s32[1]{0:T(128)} %bitcast.core, bf16[4,4,4,24,768]{4,3,2,1,0:T(8,128)(2,1)S(1)} %collective-permute-done.4.other, f32[8,768]{1,0:T(8,128)S(1)} %reshape.41.gain, bf16[4,768,768]{2,1,0:T(8,128)(2,1)S(1)} %get-tuple-element.31.weight, f32[384,768]{1,0:T(8,128)S(1)} %get-tuple-element.32.total_ref, ...), custom_call_target="tpu_custom_call" | custom-call | flops 1811939328 | bytes 12582912 | tf_op jit(solution)/shard_map/experts_second/pallas_call | solution.py:298
  65.3 0.4 collective-permute-start.6
  65.7 1.4 %collective-permute-done.6.hidden_other = bf16[384,384]{1,0:T(8,128)(2,1)S(1)} collective-permute-done((bf16[384,384]{1,0:T(8,128)(2,1)S(1)}, bf16[384,384]{1,0:T(8,128)(2,1)S(1)}, u32[]{:S(2)}, u32[]{:S(2)}) %collective-permute-start.6) | collective-permute-done | bytes 294944 | tf_op jit(solution)/shard_map/ppermute | solution.py:333
  67.1 0.0 copy-start.2
  67.1 3.2 %experts_out.1 = bf16[4,4,4,24,768]{4,3,2,1,0:T(8,128)(2,1)} custom-call(s32[1]{0:T(128)} %bitcast.core, bf16[384,384]{1,0:T(8,128)(2,1)S(1)} %experts_second.1.hidden, bf16[384,384]{1,0:T(8,128)(2,1)S(1)} %collective-permute-done.6.hidden_other, bf16[4,768,768]{2,1,0:T(8,128)(2,1)S(1)} %get-tuple-element.34.weight), custom_call_target="tpu_custom_call" | custom-call | flops 1811939328 | bytes 8388608 | tf_op jit(solution)/shard_map/experts_out/pallas_call | solution.py:315
  70.3 8.3 %all-to-all-start.1 = ((bf16[64,24,768]{2,1,0:T(8,128)(2,1)}), bf16[64,24,768]{2,1,0:T(8,128)(2,1)S(1)}, u32[]{:S(2)}, u32[]{:S(2)}) async-start(bf16[64,24,768]{2,1,0:T(8,128)(2,1)} %bitcast.12), calls=%async_computation.1 | async-start | bytes 4718592 | tf_op jit(solution)/shard_map/all_to_all | solution.py:31
  78.7 0.0 copy-done.2
  78.7 0.1 fusion.11
  78.8 29.6 %all-to-all-done.1 = bf16[64,24,768]{2,1,0:T(8,128)(2,1)S(1)} async-done(((bf16[64,24,768]{2,1,0:T(8,128)(2,1)}), bf16[64,24,768]{2,1,0:T(8,128)(2,1)S(1)}, u32[]{:S(2)}, u32[]{:S(2)}) %all-to-all-start.1) | async-done | bytes 2359328 | tf_op jit(solution)/shard_map/all_to_all | solution.py:31
  108.3 0.3 convert_reduce_fusion
  108.7 1.0 fusion
  (5 shorter events, 0.1 us)
Async XLA Ops:
  0.1 7.1 %copy-start.1 = (s32[32,2]{0,1:T(2,128)S(1)}, s32[32,2]{0,1:T(2,128)}, u32[]{:S(2)}) copy-start(s32[32,2]{0,1:T(2,128)} %param.26) | copy-start | bytes 772
  0.1 14.7 %copy-start = (f32[6144]{0:T(1024)S(1)}, f32[6144]{0:T(1024)}, u32[]{:S(2)}) copy-start(f32[6144]{0:T(1024)} %param.22) | copy-start | bytes 73732
  7.1 1.5 %collective-permute-start = (bf16[4,32,768]{2,1,0:T(8,128)(2,1)S(1)}, bf16[4,32,768]{2,1,0:T(8,128)(2,1)S(1)}, u32[]{:S(2)}, u32[]{:S(2)}) collective-permute-start(bf16[4,32,768]{2,1,0:T(8,128)(2,1)S(1)} %get-tuple-element.21), channel_id=1, source_target_pairs={{0,1},{1,0},{2,3},{3,2},{4,5},{5,4},{6,7},{7,6},{8,9},{9,8},{10,11... | collective-permute-start | bytes 589832 | tf_op jit(solution)/shard_map/ppermute | solution.py:333
  8.7 8.9 %collective-permute-start.1 = (bf16[32,768]{1,0:T(8,128)(2,1)S(1)}, bf16[32,768]{1,0:T(8,128)(2,1)S(1)}, u32[]{:S(2)}, u32[]{:S(2)}) collective-permute-start(bf16[32,768]{1,0:T(8,128)(2,1)S(1)} %get-tuple-element.39), channel_id=1, source_target_pairs={{0,2},{2,4},{4,6},{6,0},{1,3},{3,5},{5,7},{7,1},{8,10},{10,12},{12... | collective-permute-start | bytes 147464 | tf_op jit(solution)/shard_map/ppermute | solution.py:367
  10.4 7.2 %collective-permute-start.2 = (bf16[32,768]{1,0:T(8,128)(2,1)S(1)}, bf16[32,768]{1,0:T(8,128)(2,1)S(1)}, u32[]{:S(2)}, u32[]{:S(2)}) collective-permute-start(bf16[32,768]{1,0:T(8,128)(2,1)S(1)} %get-tuple-element.38), channel_id=1, source_target_pairs={{0,4},{2,6},{4,0},{6,2},{1,5},{3,7},{5,1},{7,3},{8,12},{10,14},{12... | collective-permute-start | bytes 147464 | tf_op jit(solution)/shard_map/ppermute | solution.py:367
  13.3 4.3 %collective-permute-start.3 = (bf16[32,768]{1,0:T(8,128)(2,1)S(1)}, bf16[32,768]{1,0:T(8,128)(2,1)S(1)}, u32[]{:S(2)}, u32[]{:S(2)}) collective-permute-start(bf16[32,768]{1,0:T(8,128)(2,1)S(1)} %get-tuple-element.37), channel_id=1, source_target_pairs={{0,6},{2,0},{4,2},{6,4},{1,7},{3,1},{5,3},{7,5},{8,14},{10,8},{12,... | collective-permute-start | bytes 147464 | tf_op jit(solution)/shard_map/ppermute | solution.py:367
  15.1 43.3 %collective-permute-start.5 = (bf16[384,6144]{1,0:T(8,128)(2,1)}, bf16[384,6144]{1,0:T(8,128)(2,1)S(1)}, u32[]{:S(2)}, u32[]{:S(2)}) collective-permute-start(bf16[384,6144]{1,0:T(8,128)(2,1)} %down), channel_id=1, source_target_pairs={{0,1},{1,0},{2,3},{3,2},{4,5},{5,4},{6,7},{7,6},{8,9},{9,8},{10,11... | collective-permute-start | bytes 14155784 | tf_op jit(solution)/shard_map/ppermute | solution.py:333
  58.4 4.5 %collective-permute-start.4 = (bf16[4,4,4,24,768]{4,3,2,1,0:T(8,128)(2,1)S(1)}, bf16[4,4,4,24,768]{4,3,2,1,0:T(8,128)(2,1)S(1)}, u32[]{:S(2)}, u32[]{:S(2)}) collective-permute-start(bf16[4,4,4,24,768]{4,3,2,1,0:T(8,128)(2,1)S(1)} %bitcast.32), channel_id=1, source_target_pairs={{0,1},{1,0},{2,3},{3,2},{4,5},{5,4},{6,7},{7,6},{8,9},{9,8},{10,11... | collective-permute-start | bytes 7077896 | tf_op jit(solution)/shard_map/ppermute | solution.py:333
  65.3 1.8 %collective-permute-start.6 = (bf16[384,384]{1,0:T(8,128)(2,1)S(1)}, bf16[384,384]{1,0:T(8,128)(2,1)S(1)}, u32[]{:S(2)}, u32[]{:S(2)}) collective-permute-start(bf16[384,384]{1,0:T(8,128)(2,1)S(1)} %experts_second.1.hidden), channel_id=1, source_target_pairs={{0,1},{1,0},{2,3},{3,2},{4,5},{5,4},{6,7},{7,6},{8,9},{9,8},{10,11... | collective-permute-start | bytes 884744 | tf_op jit(solution)/shard_map/ppermute | solution.py:333
  67.1 11.5 %copy-start.2 = (f32[32,2]{0,1:T(2,128)S(1)}, f32[32,2]{0,1:T(2,128)}, u32[]{:S(2)}) copy-start(f32[32,2]{0,1:T(2,128)} %param.27) | copy-start | bytes 772
  70.3 38.0 %all-to-all-start.1 = ((bf16[64,24,768]{2,1,0:T(8,128)(2,1)}), bf16[64,24,768]{2,1,0:T(8,128)(2,1)S(1)}, u32[]{:S(2)}, u32[]{:S(2)}) async-start(bf16[64,24,768]{2,1,0:T(8,128)(2,1)} %bitcast.12), calls=%async_computation.1 | async-start | bytes 4718592 | tf_op jit(solution)/shard_map/all_to_all | solution.py:31

commit v4 on v3

--- a/solution.py
+++ b/solution.py
@@ -43,12 +43,12 @@
 
 def attend_kernel(
     place, lengths, queries, new_keys, new_values, keys, values, out_weight,
-    sent_ref, kept_ref,
+    sent_ref, attended_ref, own_weight,
     length_buf, query_buf, new_key_buf, new_value_buf, key_buf, value_buf, weight_buf, sems,
 ):
     rows, head_width = new_keys.shape
     heads = queries.shape[1] // head_width
-    _, ys, _, width = weight_buf.shape
+    ys, _, width = weight_buf.shape
     span = keys.shape[2]
     parts = rows // PART
     scale = 1.0 / math.sqrt(head_width)
@@ -64,11 +64,11 @@
         for p in range(parts):
             some = pl.ds(p * PART, PART)
             copies.append((cache.at[some, 0], target.at[some]))
-    for half, side in enumerate((1 - place[0], place[0])):
+    for side, target in ((1 - place[0], weight_buf), (place[0], own_weight)):
         for step in range(ys):
             block = 2 * lax.rem(place[1] + step, ys) + side
             columns = pl.ds(pl.multiple_of(block * width, width), width)
-            copies.append((out_weight.at[:, columns], weight_buf.at[half, step]))
+            copies.append((out_weight.at[:, columns], target.at[step]))
     copies = [
         pltpu.make_async_copy(source, target, sems.at[i]) for i, (source, target) in enumerate(copies)
     ]
@@ -111,11 +111,13 @@
         attended.append(mixture + weights_new[some] * new_value[some])
     attended = jnp.concatenate(attended, axis=0).reshape(rows, heads * head_width)
     attended = attended.astype(jnp.bfloat16)
-    for half, target in enumerate((sent_ref, kept_ref)):
-        for y in range(ys):
-            copies[2 * parts + half * ys + y].wait()
-            out = jnp.dot(attended, weight_buf[half, y], preferred_element_type=jnp.float32)
-            target[y] = out.astype(target.dtype)
+    attended_ref[...] = attended
+    for y in range(ys):
+        copies[2 * parts + y].wait()
+        out = jnp.dot(attended, weight_buf[y], preferred_element_type=jnp.float32)
+        sent_ref[y] = out.astype(sent_ref.dtype)
+    for copy in copies[2 * parts + ys :]:
+        copy.wait()
 
 
 def attend(place, lengths, queries, new_keys, new_values, keys, values, out_weight):
@@ -127,10 +129,11 @@
     return pl.pallas_call(
         attend_kernel,
         in_specs=[scalars] + [outside] * 7,
-        out_specs=[inside] * 2,
+        out_specs=[inside] * 3,
         out_shape=[
             jax.ShapeDtypeStruct((ys, rows, width), jnp.bfloat16),
-            jax.ShapeDtypeStruct((ys, rows, width), jnp.float32),
+            jax.ShapeDtypeStruct((rows, width), jnp.bfloat16),
+            jax.ShapeDtypeStruct((ys, width, width), jnp.bfloat16),
         ],
         scratch_shapes=[
             pltpu.SMEM((1, rows), jnp.int32),
@@ -139,7 +142,7 @@
             pltpu.VMEM((rows, head_width), jnp.bfloat16),
             pltpu.VMEM((rows, span, head_width), jnp.bfloat16),
             pltpu.VMEM((rows, span, head_width), jnp.bfloat16),
-            pltpu.VMEM((2, ys, width, width), jnp.bfloat16),
+            pltpu.VMEM((ys, width, width), jnp.bfloat16),
             pltpu.SemaphoreType.DMA((4 + 2 * rows // PART + 2 * ys,)),
         ],
         compiler_params=pltpu.CompilerParams(vmem_limit_bytes=32 * 2**20),
@@ -148,6 +151,27 @@
         ),
         name="attend",
     )(place, *in_hbm(lengths, queries, new_keys, new_values, keys, values, out_weight))
+
+
+def project_kernel(attended, weight, out_ref):
+    for y in range(weight.shape[0]):
+        out_ref[y] = jnp.dot(attended[...], weight[y], preferred_element_type=jnp.float32)
+
+
+def project(attended, weight):
+    ys, _, width = weight.shape
+    inside = pl.BlockSpec(memory_space=pltpu.VMEM)
+    return pl.pallas_call(
+        project_kernel,
+        in_specs=[inside] * 2,
+        out_specs=inside,
+        out_shape=jax.ShapeDtypeStruct((ys, attended.shape[0], width), jnp.float32),
+        compiler_params=pltpu.CompilerParams(vmem_limit_bytes=16 * 2**20),
+        cost_estimate=pl.CostEstimate(
+            flops=attended.size * width * 8, bytes_accessed=5 * 2**20, transcendentals=0
+        ),
+        name="project",
+    )(attended, weight)
 
 
 def gate_up_copies(side, gate, up, target, sems):
@@ -358,9 +382,13 @@
 
     core_index = core.astype(jnp.int32).reshape(1)
     place = jnp.stack([core, lax.axis_index("y")]).astype(jnp.int32)
-    sent, kept = attend(
+    order = jnp.arange(EXPERTS) ^ (FLIP * core)
+    start = column * share
+    queries, order, start = lax.optimization_barrier((queries, order, start))
+    sent, attended, own_columns = attend(
         place, cache_lengths.reshape(1, -1), queries, new_keys, new_values, key_cache, value_cache, out_weight
     )
+    kept = project(attended, own_columns)
     first = kept + swap(sent).astype(jnp.float32)
     chips_y = lax.axis_size("y")
     pieces = [
@@ -376,13 +404,11 @@
     down_other = swap(down_weight)
     own_weight = load_weights(core_index, gate_weight, up_weight)
     pieces, own_weight = lax.optimization_barrier((pieces, own_weight))
-    start = column * share
     middle = lax.dynamic_slice_in_dim(residual, start, share, 1).astype(jnp.float32)
     middle = middle + first[0] + sum(piece.astype(jnp.float32) for piece in pieces)
     gain = lax.dynamic_slice_in_dim(norm_gain, start, share, 0)
     gained = (middle * gain).astype(jnp.bfloat16)
 
-    order = jnp.arange(EXPERTS) ^ (FLIP * core)
     named = routes[:, :, None] == order[None, None, :]
     coef = jnp.sum(jnp.where(named, route_gates[:, :, None], 0.0), axis=1)
     taken = jnp.any(named, axis=1)

time: 110 us -> 109 us (level)
  transfers between devices with their start and end apart: 8 -> 8, of which waited for: 4 -> 4; matrix products, arithmetic and copies ran while one was open for 2% -> 2% of each run, Pallas kernels for 5% -> 6%
where the time goes in v4:
time: 109 us
  blocking collectives  39.6 us (36%)
  waiting for transfers between devices  32.7 us (30%)
  Pallas kernels  18 us (17%)
  starting transfers between devices  14.8 us (14%)
  other arithmetic  1.6 us (1%)
  matrix products  1.26 us (1%)
    all_to_all x1, blocking collectives, exchange(): lax.all_to_all(flat, EVERY, split_axis=0, concat_axis=0, axis_index_group...  39.6 us
    all_to_all x1, waiting for transfers between devices, exchange(): lax.all_to_all(flat, EVERY, split_axis=0, concat_axis=0, axis_index_group...  29.6 us
    all_to_all x1, starting transfers between devices, exchange(): lax.all_to_all(flat, EVERY, split_axis=0, concat_axis=0, axis_index_group...  8.37 us
    pallas_call x1, Pallas kernels, attend(): pl.pallas_call(attend_kernel, in_specs=[scalars] + [outside] * 7, out_spe...  6.02 us
    ppermute x3, starting transfers between devices, layer_block(): lax.ppermute(first[s].astype(jnp.bfloat16), 'y', [(i, (i + s) % chips_y)...  5.98 us
    pallas_call x1, Pallas kernels, experts_first(): pl.pallas_call(first_kernel, in_specs=[pl.BlockSpec(memory_space=pltpu.SM...  3.2 us
    pallas_call x1, Pallas kernels, experts_out(): pl.pallas_call(out_kernel, in_specs=[pl.BlockSpec(memory_space=pltpu.SMEM...  3.18 us
    ppermute x4, waiting for transfers between devices, swap(): return lax.ppermute(value, 'core', [(0, 1), (1, 0)])  3.18 us
  transfers between devices with their start and end apart: 8, of which 4 were waited for; matrix products, arithmetic and copies ran while one was open for 2% of the time, Pallas kernels for 6%

profile of v4, /device:TPU:0, one launch (start us, length us, event | category | flops | bytes accessed | tf_op | source)
XLA Modules:
  0.0 108.5 jit_solution(1125882708812423364)
XLA Ops:
  0.0 0.1 pad_add_fusion.place
  0.1 6.0 %attend.1 = (bf16[4,32,768]{2,1,0:T(8,128)(2,1)S(1)}, bf16[32,768]{1,0:T(8,128)(2,1)S(1)}, bf16[4,768,768]{2,1,0:T(8,128)(2,1)S(1)}) custom-call(s32[2]{0:T(128)S(1)} %pad_add_fusion.place, s32[1,32]{1,0:T(1,128)} %bitcast.37, bf16[32,768]{1,0:T(8,128)(2,1)} %queries, bf16[32,128]{1,0:T(8,128)(2,1)} %new_keys.1, bf16[32,128]{1,0:T(8,128)(2,1)} %new_values.1, ...), custom_call_target="tpu_custom_call" | custom-call | flops 150994944 | bytes 15728640 | tf_op jit(solution)/shard_map/attend/pallas_call | solution.py:129
  6.1 0.0 copy-start.1
  6.1 0.0 copy-start
  6.1 0.1 collective-permute-start
  6.2 0.9 project.1
  7.1 0.0 copy-done.1
  7.1 0.1 compare_reduce_fusion
  7.2 0.4 collective-permute-done
  7.7 1.7 %collective-permute-start.1 = (bf16[32,768]{1,0:T(8,128)(2,1)S(1)}, bf16[32,768]{1,0:T(8,128)(2,1)S(1)}, u32[]{:S(2)}, u32[]{:S(2)}) collective-permute-start(bf16[32,768]{1,0:T(8,128)(2,1)S(1)} %get-tuple-element.47), channel_id=1, source_target_pairs={{0,2},{2,4},{4,6},{6,0},{1,3},{3,5},{5,7},{7,1},{8,10},{10,12},{12... | collective-permute-start | bytes 147464 | tf_op jit(solution)/shard_map/ppermute | solution.py:395
  9.5 2.9 %collective-permute-start.2 = (bf16[32,768]{1,0:T(8,128)(2,1)S(1)}, bf16[32,768]{1,0:T(8,128)(2,1)S(1)}, u32[]{:S(2)}, u32[]{:S(2)}) collective-permute-start(bf16[32,768]{1,0:T(8,128)(2,1)S(1)} %get-tuple-element.46), channel_id=1, source_target_pairs={{0,4},{2,6},{4,0},{6,2},{1,5},{3,7},{5,1},{7,3},{8,12},{10,14},{12... | collective-permute-start | bytes 147464 | tf_op jit(solution)/shard_map/ppermute | solution.py:395
  12.4 1.3 %collective-permute-start.3 = (bf16[32,768]{1,0:T(8,128)(2,1)S(1)}, bf16[32,768]{1,0:T(8,128)(2,1)S(1)}, u32[]{:S(2)}, u32[]{:S(2)}) collective-permute-start(bf16[32,768]{1,0:T(8,128)(2,1)S(1)} %get-tuple-element.45), channel_id=1, source_target_pairs={{0,6},{2,0},{4,2},{6,4},{1,7},{3,1},{5,3},{7,5},{8,14},{10,8},{12,... | collective-permute-start | bytes 147464 | tf_op jit(solution)/shard_map/ppermute | solution.py:395
  13.7 0.1 convolution_convert_fusion.1
  13.8 0.0 copy-done
  13.8 0.1 dynamic_slice.7
  13.9 0.1 eq.45
  14.0 0.1 fusion.6
  14.1 0.1 collective-permute-start.5
  14.2 2.4 %load_weights.1.weight = bf16[4,768,768]{2,1,0:T(8,128)(2,1)S(1)} custom-call(s32[1]{0:T(128)} %bitcast.core, bf16[6144,384]{1,0:T(8,128)(2,1)} %gate.1, bf16[6144,384]{1,0:T(8,128)(2,1)} %up.1), custom_call_target="tpu_custom_call" | custom-call | bytes 9437184 | tf_op jit(solution)/shard_map/load_weights/pallas_call | solution.py:199
  16.6 0.0 collective-permute-done.1
  16.6 0.0 collective-permute-done.2
  16.6 0.0 collective-permute-done.3
  16.6 0.9 fusion.1
  17.5 0.2 convolution_convert_fusion
  17.7 0.2 broadcast_in_dim.46
  17.9 39.6 %all_to_all.10 = bf16[64,24,768]{2,1,0:T(8,128)(2,1)S(1)} all-to-all(bf16[64,24,768]{2,1,0:T(8,128)(2,1)S(1)} %bitcast.35), channel_id=1, replica_groups={{0,8,16,24,32,40,48,56,64,72,80,88,96,104,112,120,2,10,18,26,34,42,50,5..., dimensions={0} | all-to-all | bytes 4718592 | tf_op jit(solution)/shard_map/all_to_all | solution.py:31
  57.5 0.0 collective-permute-start.4
  57.5 0.0 collective-permute-done.5.down_other
  57.5 3.2 %experts_first.1 = (f32[384,768]{1,0:T(8,128)S(1)}, f32[384,128]{1,0:T(8,128)S(1)}, bf16[4,768,768]{2,1,0:T(8,128)(2,1)S(1)}, bf16[4,768,768]{2,1,0:T(8,128)(2,1)S(1)}) custom-call(s32[1]{0:T(128)} %bitcast.core, bf16[4,4,4,24,768]{4,3,2,1,0:T(8,128)(2,1)S(1)} %bitcast.33, f32[8,768]{1,0:T(8,128)S(1)} %reshape.38.gain, ...), custom_call_target="tpu_custom_call" | custom-call | flops 1811939328 | bytes 12582912 | tf_op jit(solution)/shard_map/experts_first/pallas_call | solution.py:299
  60.7 1.3 %collective-permute-done.4.other = bf16[4,4,4,24,768]{4,3,2,1,0:T(8,128)(2,1)S(1)} collective-permute-done((bf16[4,4,4,24,768]{4,3,2,1,0:T(8,128)(2,1)S(1)}, bf16[4,4,4,24,768]{4,3,2,1,0:T(8,128)(2,1)S(1)}, u32[]{:S(2)}, u32[]{:S(2)}) %collective-permute-start.4) | collective-permute-done | bytes 2359328 | tf_op jit(solution)/shard_map/ppermute | solution.py:357
  62.0 2.3 %experts_second.1.hidden = bf16[384,384]{1,0:T(8,128)(2,1)S(1)} custom-call(s32[1]{0:T(128)} %bitcast.core, bf16[4,4,4,24,768]{4,3,2,1,0:T(8,128)(2,1)S(1)} %collective-permute-done.4.other, f32[8,768]{1,0:T(8,128)S(1)} %reshape.38.gain, bf16[4,768,768]{2,1,0:T(8,128)(2,1)S(1)} %get-tuple-element.39.weight, f32[384,768]{1,0:T(8,128)S(1)} %get-tuple-element.40.total_ref, ...), custom_call_target="tpu_custom_call" | custom-call | flops 1811939328 | bytes 12582912 | tf_op jit(solution)/shard_map/experts_second/pallas_call | solution.py:322
  64.4 0.2 collective-permute-start.6
  64.6 1.4 %collective-permute-done.6.hidden_other = bf16[384,384]{1,0:T(8,128)(2,1)S(1)} collective-permute-done((bf16[384,384]{1,0:T(8,128)(2,1)S(1)}, bf16[384,384]{1,0:T(8,128)(2,1)S(1)}, u32[]{:S(2)}, u32[]{:S(2)}) %collective-permute-start.6) | collective-permute-done | bytes 294944 | tf_op jit(solution)/shard_map/ppermute | solution.py:357
  66.0 0.0 copy-start.2
  66.0 3.2 %experts_out.1 = bf16[4,4,4,24,768]{4,3,2,1,0:T(8,128)(2,1)} custom-call(s32[1]{0:T(128)} %bitcast.core, bf16[384,384]{1,0:T(8,128)(2,1)S(1)} %experts_second.1.hidden, bf16[384,384]{1,0:T(8,128)(2,1)S(1)} %collective-permute-done.6.hidden_other, bf16[4,768,768]{2,1,0:T(8,128)(2,1)S(1)} %get-tuple-element.42.weight), custom_call_target="tpu_custom_call" | custom-call | flops 1811939328 | bytes 8388608 | tf_op jit(solution)/shard_map/experts_out/pallas_call | solution.py:339
  69.2 8.4 %all-to-all-start.1 = ((bf16[64,24,768]{2,1,0:T(8,128)(2,1)}), bf16[64,24,768]{2,1,0:T(8,128)(2,1)S(1)}, u32[]{:S(2)}, u32[]{:S(2)}) async-start(bf16[64,24,768]{2,1,0:T(8,128)(2,1)} %bitcast.12), calls=%async_computation.1 | async-start | bytes 4718592 | tf_op jit(solution)/shard_map/all_to_all | solution.py:31
  77.6 0.0 copy-done.2
  77.6 0.1 fusion.11
  77.7 29.6 %all-to-all-done.1 = bf16[64,24,768]{2,1,0:T(8,128)(2,1)S(1)} async-done(((bf16[64,24,768]{2,1,0:T(8,128)(2,1)}), bf16[64,24,768]{2,1,0:T(8,128)(2,1)S(1)}, u32[]{:S(2)}, u32[]{:S(2)}) %all-to-all-start.1) | async-done | bytes 2359328 | tf_op jit(solution)/shard_map/all_to_all | solution.py:31
  107.3 0.3 convert_reduce_fusion
  107.6 1.0 fusion
  (5 shorter events, 0.1 us)
Async XLA Ops:
  6.1 1.0 copy-start.1
  6.1 7.7 %copy-start = (f32[6144]{0:T(1024)S(1)}, f32[6144]{0:T(1024)}, u32[]{:S(2)}) copy-start(f32[6144]{0:T(1024)} %param.22) | copy-start | bytes 73732
  6.1 1.5 %collective-permute-start = (bf16[4,32,768]{2,1,0:T(8,128)(2,1)S(1)}, bf16[4,32,768]{2,1,0:T(8,128)(2,1)S(1)}, u32[]{:S(2)}, u32[]{:S(2)}) collective-permute-start(bf16[4,32,768]{2,1,0:T(8,128)(2,1)S(1)} %get-tuple-element.28), channel_id=1, source_target_pairs={{0,1},{1,0},{2,3},{3,2},{4,5},{5,4},{6,7},{7,6},{8,9},{9,8},{10,11... | collective-permute-start | bytes 589832 | tf_op jit(solution)/shard_map/ppermute | solution.py:357
  7.7 8.9 %collective-permute-start.1 = (bf16[32,768]{1,0:T(8,128)(2,1)S(1)}, bf16[32,768]{1,0:T(8,128)(2,1)S(1)}, u32[]{:S(2)}, u32[]{:S(2)}) collective-permute-start(bf16[32,768]{1,0:T(8,128)(2,1)S(1)} %get-tuple-element.47), channel_id=1, source_target_pairs={{0,2},{2,4},{4,6},{6,0},{1,3},{3,5},{5,7},{7,1},{8,10},{10,12},{12... | collective-permute-start | bytes 147464 | tf_op jit(solution)/shard_map/ppermute | solution.py:395
  9.5 7.2 %collective-permute-start.2 = (bf16[32,768]{1,0:T(8,128)(2,1)S(1)}, bf16[32,768]{1,0:T(8,128)(2,1)S(1)}, u32[]{:S(2)}, u32[]{:S(2)}) collective-permute-start(bf16[32,768]{1,0:T(8,128)(2,1)S(1)} %get-tuple-element.46), channel_id=1, source_target_pairs={{0,4},{2,6},{4,0},{6,2},{1,5},{3,7},{5,1},{7,3},{8,12},{10,14},{12... | collective-permute-start | bytes 147464 | tf_op jit(solution)/shard_map/ppermute | solution.py:395
  12.4 4.3 %collective-permute-start.3 = (bf16[32,768]{1,0:T(8,128)(2,1)S(1)}, bf16[32,768]{1,0:T(8,128)(2,1)S(1)}, u32[]{:S(2)}, u32[]{:S(2)}) collective-permute-start(bf16[32,768]{1,0:T(8,128)(2,1)S(1)} %get-tuple-element.45), channel_id=1, source_target_pairs={{0,6},{2,0},{4,2},{6,4},{1,7},{3,1},{5,3},{7,5},{8,14},{10,8},{12,... | collective-permute-start | bytes 147464 | tf_op jit(solution)/shard_map/ppermute | solution.py:395
  14.1 43.4 %collective-permute-start.5 = (bf16[384,6144]{1,0:T(8,128)(2,1)}, bf16[384,6144]{1,0:T(8,128)(2,1)S(1)}, u32[]{:S(2)}, u32[]{:S(2)}) collective-permute-start(bf16[384,6144]{1,0:T(8,128)(2,1)} %down), channel_id=1, source_target_pairs={{0,1},{1,0},{2,3},{3,2},{4,5},{5,4},{6,7},{7,6},{8,9},{9,8},{10,11... | collective-permute-start | bytes 14155784 | tf_op jit(solution)/shard_map/ppermute | solution.py:357
  57.5 4.5 %collective-permute-start.4 = (bf16[4,4,4,24,768]{4,3,2,1,0:T(8,128)(2,1)S(1)}, bf16[4,4,4,24,768]{4,3,2,1,0:T(8,128)(2,1)S(1)}, u32[]{:S(2)}, u32[]{:S(2)}) collective-permute-start(bf16[4,4,4,24,768]{4,3,2,1,0:T(8,128)(2,1)S(1)} %bitcast.32), channel_id=1, source_target_pairs={{0,1},{1,0},{2,3},{3,2},{4,5},{5,4},{6,7},{7,6},{8,9},{9,8},{10,11... | collective-permute-start | bytes 7077896 | tf_op jit(solution)/shard_map/ppermute | solution.py:357
  64.4 1.7 %collective-permute-start.6 = (bf16[384,384]{1,0:T(8,128)(2,1)S(1)}, bf16[384,384]{1,0:T(8,128)(2,1)S(1)}, u32[]{:S(2)}, u32[]{:S(2)}) collective-permute-start(bf16[384,384]{1,0:T(8,128)(2,1)S(1)} %experts_second.1.hidden), channel_id=1, source_target_pairs={{0,1},{1,0},{2,3},{3,2},{4,5},{5,4},{6,7},{7,6},{8,9},{9,8},{10,11... | collective-permute-start | bytes 884744 | tf_op jit(solution)/shard_map/ppermute | solution.py:357
  66.0 11.6 %copy-start.2 = (f32[32,2]{0,1:T(2,128)S(1)}, f32[32,2]{0,1:T(2,128)}, u32[]{:S(2)}) copy-start(f32[32,2]{0,1:T(2,128)} %param.27) | copy-start | bytes 772
  69.2 38.0 %all-to-all-start.1 = ((bf16[64,24,768]{2,1,0:T(8,128)(2,1)}), bf16[64,24,768]{2,1,0:T(8,128)(2,1)S(1)}, u32[]{:S(2)}, u32[]{:S(2)}) async-start(bf16[64,24,768]{2,1,0:T(8,128)(2,1)} %bitcast.12), calls=%async_computation.1 | async-start | bytes 4718592 | tf_op jit(solution)/shard_map/all_to_all | solution.py:31

commit v5 on v4

--- a/solution.py
+++ b/solution.py
@@ -383,12 +383,17 @@
     core_index = core.astype(jnp.int32).reshape(1)
     place = jnp.stack([core, lax.axis_index("y")]).astype(jnp.int32)
     order = jnp.arange(EXPERTS) ^ (FLIP * core)
-    start = column * share
+    start = (column * share).astype(jnp.uint32)
     queries, order, start = lax.optimization_barrier((queries, order, start))
     sent, attended, own_columns = attend(
         place, cache_lengths.reshape(1, -1), queries, new_keys, new_values, key_cache, value_cache, out_weight
     )
-    kept = project(attended, own_columns)
+    kept, mine = lax.optimization_barrier(
+        (
+            project(attended, own_columns),
+            lax.dynamic_slice(residual, (jnp.uint32(0), start), (rows, share)),
+        )
+    )
     first = kept + swap(sent).astype(jnp.float32)
     chips_y = lax.axis_size("y")
     pieces = [
@@ -404,9 +409,8 @@
     down_other = swap(down_weight)
     own_weight = load_weights(core_index, gate_weight, up_weight)
     pieces, own_weight = lax.optimization_barrier((pieces, own_weight))
-    middle = lax.dynamic_slice_in_dim(residual, start, share, 1).astype(jnp.float32)
-    middle = middle + first[0] + sum(piece.astype(jnp.float32) for piece in pieces)
-    gain = lax.dynamic_slice_in_dim(norm_gain, start, share, 0)
+    middle = mine.astype(jnp.float32) + first[0] + sum(piece.astype(jnp.float32) for piece in pieces)
+    gain = lax.dynamic_slice(norm_gain, (start,), (share,))
     gained = (middle * gain).astype(jnp.bfloat16)
 
     named = routes[:, :, None] == order[None, None, :]
@@ -432,7 +436,7 @@
     outs = experts_out(core_index, hidden, swap(hidden), out_weights, shape)
     returned = exchange(outs)
     merged = jnp.sum(returned.astype(jnp.float32), axis=(0, 2)).reshape(EXPERTS * CAP, share)
-    return middle + jnp.dot(blend, merged, precision=lax.Precision.HIGHEST)
+    return middle + jnp.dot(blend, merged, precision=lax.Precision.HIGH)
 
 
 def solution(mesh):

time: 109 us -> 108 us (level)
  transfers between devices with their start and end apart: 8 -> 8, of which waited for: 4 -> 4; matrix products, arithmetic and copies ran while one was open for 2% -> 1% of each run, Pallas kernels for 6% -> 6%
where the time goes in v5:
time: 108 us
  blocking collectives  39.6 us (37%)
  waiting for transfers between devices  32.5 us (30%)
  Pallas kernels  18 us (17%)
  starting transfers between devices  14.8 us (14%)
  matrix products  1.22 us (1%)
    all_to_all x1, blocking collectives, exchange(): lax.all_to_all(flat, EVERY, split_axis=0, concat_axis=0, axis_index_group...  39.6 us
    all_to_all x1, waiting for transfers between devices, exchange(): lax.all_to_all(flat, EVERY, split_axis=0, concat_axis=0, axis_index_group...  29.4 us
    all_to_all x1, starting transfers between devices, exchange(): lax.all_to_all(flat, EVERY, split_axis=0, concat_axis=0, axis_index_group...  8.43 us
    pallas_call x1, Pallas kernels, attend(): pl.pallas_call(attend_kernel, in_specs=[scalars] + [outside] * 7, out_spe...  6.02 us
    ppermute x3, starting transfers between devices, layer_block(): lax.ppermute(first[s].astype(jnp.bfloat16), 'y', [(i, (i + s) % chips_y)...  5.98 us
    pallas_call x1, Pallas kernels, experts_first(): pl.pallas_call(first_kernel, in_specs=[pl.BlockSpec(memory_space=pltpu.SM...  3.2 us
    pallas_call x1, Pallas kernels, experts_out(): pl.pallas_call(out_kernel, in_specs=[pl.BlockSpec(memory_space=pltpu.SMEM...  3.18 us
    ppermute x4, waiting for transfers between devices, swap(): return lax.ppermute(value, 'core', [(0, 1), (1, 0)])  3.09 us
  transfers between devices with their start and end apart: 8, of which 4 were waited for; matrix products, arithmetic and copies ran while one was open for 1% of the time, Pallas kernels for 6%

profile of v5, /device:TPU:0, one launch (start us, length us, event | category | flops | bytes accessed | tf_op | source)
XLA Modules:
  0.0 107.5 jit_solution(7973095271310819321)
XLA Ops:
  0.0 0.0 copy-start
  0.0 0.1 pad_add_fusion.place
  0.1 6.0 %attend.1 = (bf16[4,32,768]{2,1,0:T(8,128)(2,1)S(1)}, bf16[32,768]{1,0:T(8,128)(2,1)S(1)}, bf16[4,768,768]{2,1,0:T(8,128)(2,1)S(1)}) custom-call(s32[2]{0:T(128)S(1)} %pad_add_fusion.place, s32[1,32]{1,0:T(1,128)} %bitcast.42, bf16[32,768]{1,0:T(8,128)(2,1)} %queries, bf16[32,128]{1,0:T(8,128)(2,1)} %new_keys.1, bf16[32,128]{1,0:T(8,128)(2,1)} %new_values.1, ...), custom_call_target="tpu_custom_call" | custom-call | flops 150994944 | bytes 15728640 | tf_op jit(solution)/shard_map/attend/pallas_call | solution.py:129
  6.1 0.0 copy-start.3
  6.1 0.0 copy-start.2
  6.1 0.1 collective-permute-start
  6.2 0.9 project.1
  7.1 0.0 copy-done
  7.1 0.1 constant_dynamic-slice_fusion
  7.2 0.0 copy-done.3
  7.2 0.1 compare_reduce_fusion
  7.3 0.3 collective-permute-done
  7.7 1.7 %collective-permute-start.1 = (bf16[32,768]{1,0:T(8,128)(2,1)S(1)}, bf16[32,768]{1,0:T(8,128)(2,1)S(1)}, u32[]{:S(2)}, u32[]{:S(2)}) collective-permute-start(bf16[32,768]{1,0:T(8,128)(2,1)S(1)} %get-tuple-element.51), channel_id=1, source_target_pairs={{0,2},{2,4},{4,6},{6,0},{1,3},{3,5},{5,7},{7,1},{8,10},{10,12},{12... | collective-permute-start | bytes 147464 | tf_op jit(solution)/shard_map/ppermute | solution.py:400
  9.5 2.9 %collective-permute-start.2 = (bf16[32,768]{1,0:T(8,128)(2,1)S(1)}, bf16[32,768]{1,0:T(8,128)(2,1)S(1)}, u32[]{:S(2)}, u32[]{:S(2)}) collective-permute-start(bf16[32,768]{1,0:T(8,128)(2,1)S(1)} %get-tuple-element.50), channel_id=1, source_target_pairs={{0,4},{2,6},{4,0},{6,2},{1,5},{3,7},{5,1},{7,3},{8,12},{10,14},{12... | collective-permute-start | bytes 147464 | tf_op jit(solution)/shard_map/ppermute | solution.py:400
  12.4 1.3 %collective-permute-start.3 = (bf16[32,768]{1,0:T(8,128)(2,1)S(1)}, bf16[32,768]{1,0:T(8,128)(2,1)S(1)}, u32[]{:S(2)}, u32[]{:S(2)}) collective-permute-start(bf16[32,768]{1,0:T(8,128)(2,1)S(1)} %get-tuple-element.49), channel_id=1, source_target_pairs={{0,6},{2,0},{4,2},{6,4},{1,7},{3,1},{5,3},{7,5},{8,14},{10,8},{12,... | collective-permute-start | bytes 147464 | tf_op jit(solution)/shard_map/ppermute | solution.py:400
  13.7 0.1 convolution_convert_fusion.1
  13.8 0.0 copy-done.2
  13.9 0.1 dynamic_slice.7
  13.9 0.1 eq.45
  14.0 0.1 fusion.6
  14.1 0.1 collective-permute-start.5
  14.2 2.4 %load_weights.1.weight = bf16[4,768,768]{2,1,0:T(8,128)(2,1)S(1)} custom-call(s32[1]{0:T(128)} %bitcast.core, bf16[6144,384]{1,0:T(8,128)(2,1)} %gate.1, bf16[6144,384]{1,0:T(8,128)(2,1)} %up.1), custom_call_target="tpu_custom_call" | custom-call | bytes 9437184 | tf_op jit(solution)/shard_map/load_weights/pallas_call | solution.py:199
  16.6 0.0 collective-permute-done.1
  16.6 0.0 collective-permute-done.2
  16.6 0.0 collective-permute-done.3
  16.6 0.2 convolution_convert_fusion
  16.8 0.2 broadcast_in_dim.46
  17.0 39.6 %all_to_all.10 = bf16[64,24,768]{2,1,0:T(8,128)(2,1)S(1)} all-to-all(bf16[64,24,768]{2,1,0:T(8,128)(2,1)S(1)} %bitcast.40), channel_id=1, replica_groups={{0,8,16,24,32,40,48,56,64,72,80,88,96,104,112,120,2,10,18,26,34,42,50,5..., dimensions={0} | all-to-all | bytes 4718592 | tf_op jit(solution)/shard_map/all_to_all | solution.py:31
  56.6 0.0 collective-permute-start.4
  56.6 0.0 collective-permute-done.5.down_other
  56.6 3.2 %experts_first.1 = (f32[384,768]{1,0:T(8,128)S(1)}, f32[384,128]{1,0:T(8,128)S(1)}, bf16[4,768,768]{2,1,0:T(8,128)(2,1)S(1)}, bf16[4,768,768]{2,1,0:T(8,128)(2,1)S(1)}) custom-call(s32[1]{0:T(128)} %bitcast.core, bf16[4,4,4,24,768]{4,3,2,1,0:T(8,128)(2,1)S(1)} %bitcast.38, f32[8,768]{1,0:T(8,128)S(1)} %reshape.38.gain, ...), custom_call_target="tpu_custom_call" | custom-call | flops 1811939328 | bytes 12582912 | tf_op jit(solution)/shard_map/experts_first/pallas_call | solution.py:299
  59.8 1.3 %collective-permute-done.4.other = bf16[4,4,4,24,768]{4,3,2,1,0:T(8,128)(2,1)S(1)} collective-permute-done((bf16[4,4,4,24,768]{4,3,2,1,0:T(8,128)(2,1)S(1)}, bf16[4,4,4,24,768]{4,3,2,1,0:T(8,128)(2,1)S(1)}, u32[]{:S(2)}, u32[]{:S(2)}) %collective-permute-start.4) | collective-permute-done | bytes 2359328 | tf_op jit(solution)/shard_map/ppermute | solution.py:357
  61.1 2.4 %experts_second.1.hidden = bf16[384,384]{1,0:T(8,128)(2,1)S(1)} custom-call(s32[1]{0:T(128)} %bitcast.core, bf16[4,4,4,24,768]{4,3,2,1,0:T(8,128)(2,1)S(1)} %collective-permute-done.4.other, f32[8,768]{1,0:T(8,128)S(1)} %reshape.38.gain, bf16[4,768,768]{2,1,0:T(8,128)(2,1)S(1)} %get-tuple-element.43.weight, f32[384,768]{1,0:T(8,128)S(1)} %get-tuple-element.44.total_ref, ...), custom_call_target="tpu_custom_call" | custom-call | flops 1811939328 | bytes 12582912 | tf_op jit(solution)/shard_map/experts_second/pallas_call | solution.py:322
  63.5 0.2 collective-permute-start.6
  63.7 1.4 %collective-permute-done.6.hidden_other = bf16[384,384]{1,0:T(8,128)(2,1)S(1)} collective-permute-done((bf16[384,384]{1,0:T(8,128)(2,1)S(1)}, bf16[384,384]{1,0:T(8,128)(2,1)S(1)}, u32[]{:S(2)}, u32[]{:S(2)}) %collective-permute-start.6) | collective-permute-done | bytes 294944 | tf_op jit(solution)/shard_map/ppermute | solution.py:357
  65.1 0.0 copy-start.4
  65.1 0.0 copy-start.1
  65.1 3.2 %experts_out.1 = bf16[4,4,4,24,768]{4,3,2,1,0:T(8,128)(2,1)} custom-call(s32[1]{0:T(128)} %bitcast.core, bf16[384,384]{1,0:T(8,128)(2,1)S(1)} %experts_second.1.hidden, bf16[384,384]{1,0:T(8,128)(2,1)S(1)} %collective-permute-done.6.hidden_other, bf16[4,768,768]{2,1,0:T(8,128)(2,1)S(1)} %get-tuple-element.46.weight), custom_call_target="tpu_custom_call" | custom-call | flops 1811939328 | bytes 8388608 | tf_op jit(solution)/shard_map/experts_out/pallas_call | solution.py:339
  68.3 8.4 %all-to-all-start.1 = ((bf16[64,24,768]{2,1,0:T(8,128)(2,1)}), bf16[64,24,768]{2,1,0:T(8,128)(2,1)S(1)}, u32[]{:S(2)}, u32[]{:S(2)}) async-start(bf16[64,24,768]{2,1,0:T(8,128)(2,1)} %bitcast.12), calls=%async_computation.1 | async-start | bytes 4718592 | tf_op jit(solution)/shard_map/all_to_all | solution.py:31
  76.8 0.0 copy-done.4
  76.8 0.1 fusion.11
  76.9 29.4 %all-to-all-done.1 = bf16[64,24,768]{2,1,0:T(8,128)(2,1)S(1)} async-done(((bf16[64,24,768]{2,1,0:T(8,128)(2,1)}), bf16[64,24,768]{2,1,0:T(8,128)(2,1)S(1)}, u32[]{:S(2)}, u32[]{:S(2)}) %all-to-all-start.1) | async-done | bytes 2359328 | tf_op jit(solution)/shard_map/all_to_all | solution.py:31
  106.3 0.3 convert_reduce_fusion
  106.6 0.9 fusion
  107.5 0.0 copy-done.1
  (5 shorter events, 0.1 us)
Async XLA Ops:
  0.0 7.1 %copy-start = (bf16[32,6144]{1,0:T(8,128)(2,1)S(1)}, bf16[32,6144]{1,0:T(8,128)(2,1)}, u32[]{:S(2)}) copy-start(bf16[32,6144]{1,0:T(8,128)(2,1)} %param.14) | copy-start | bytes 1179652
  6.1 1.1 %copy-start.3 = (s32[32,2]{0,1:T(2,128)S(1)}, s32[32,2]{0,1:T(2,128)}, u32[]{:S(2)}) copy-start(s32[32,2]{0,1:T(2,128)} %param.26) | copy-start | bytes 772
  6.1 7.7 %copy-start.2 = (f32[6144]{0:T(1024)S(1)}, f32[6144]{0:T(1024)}, u32[]{:S(2)}) copy-start(f32[6144]{0:T(1024)} %param.22) | copy-start | bytes 73732
  6.1 1.5 %collective-permute-start = (bf16[4,32,768]{2,1,0:T(8,128)(2,1)S(1)}, bf16[4,32,768]{2,1,0:T(8,128)(2,1)S(1)}, u32[]{:S(2)}, u32[]{:S(2)}) collective-permute-start(bf16[4,32,768]{2,1,0:T(8,128)(2,1)S(1)} %get-tuple-element.32), channel_id=1, source_target_pairs={{0,1},{1,0},{2,3},{3,2},{4,5},{5,4},{6,7},{7,6},{8,9},{9,8},{10,11... | collective-permute-start | bytes 589832 | tf_op jit(solution)/shard_map/ppermute | solution.py:357
  7.7 8.9 %collective-permute-start.1 = (bf16[32,768]{1,0:T(8,128)(2,1)S(1)}, bf16[32,768]{1,0:T(8,128)(2,1)S(1)}, u32[]{:S(2)}, u32[]{:S(2)}) collective-permute-start(bf16[32,768]{1,0:T(8,128)(2,1)S(1)} %get-tuple-element.51), channel_id=1, source_target_pairs={{0,2},{2,4},{4,6},{6,0},{1,3},{3,5},{5,7},{7,1},{8,10},{10,12},{12... | collective-permute-start | bytes 147464 | tf_op jit(solution)/shard_map/ppermute | solution.py:400
  9.5 7.2 %collective-permute-start.2 = (bf16[32,768]{1,0:T(8,128)(2,1)S(1)}, bf16[32,768]{1,0:T(8,128)(2,1)S(1)}, u32[]{:S(2)}, u32[]{:S(2)}) collective-permute-start(bf16[32,768]{1,0:T(8,128)(2,1)S(1)} %get-tuple-element.50), channel_id=1, source_target_pairs={{0,4},{2,6},{4,0},{6,2},{1,5},{3,7},{5,1},{7,3},{8,12},{10,14},{12... | collective-permute-start | bytes 147464 | tf_op jit(solution)/shard_map/ppermute | solution.py:400
  12.4 4.3 %collective-permute-start.3 = (bf16[32,768]{1,0:T(8,128)(2,1)S(1)}, bf16[32,768]{1,0:T(8,128)(2,1)S(1)}, u32[]{:S(2)}, u32[]{:S(2)}) collective-permute-start(bf16[32,768]{1,0:T(8,128)(2,1)S(1)} %get-tuple-element.49), channel_id=1, source_target_pairs={{0,6},{2,0},{4,2},{6,4},{1,7},{3,1},{5,3},{7,5},{8,14},{10,8},{12,... | collective-permute-start | bytes 147464 | tf_op jit(solution)/shard_map/ppermute | solution.py:400
  14.1 42.5 %collective-permute-start.5 = (bf16[384,6144]{1,0:T(8,128)(2,1)}, bf16[384,6144]{1,0:T(8,128)(2,1)S(1)}, u32[]{:S(2)}, u32[]{:S(2)}) collective-permute-start(bf16[384,6144]{1,0:T(8,128)(2,1)} %down), channel_id=1, source_target_pairs={{0,1},{1,0},{2,3},{3,2},{4,5},{5,4},{6,7},{7,6},{8,9},{9,8},{10,11... | collective-permute-start | bytes 14155784 | tf_op jit(solution)/shard_map/ppermute | solution.py:357
  56.6 4.5 %collective-permute-start.4 = (bf16[4,4,4,24,768]{4,3,2,1,0:T(8,128)(2,1)S(1)}, bf16[4,4,4,24,768]{4,3,2,1,0:T(8,128)(2,1)S(1)}, u32[]{:S(2)}, u32[]{:S(2)}) collective-permute-start(bf16[4,4,4,24,768]{4,3,2,1,0:T(8,128)(2,1)S(1)} %bitcast.37), channel_id=1, source_target_pairs={{0,1},{1,0},{2,3},{3,2},{4,5},{5,4},{6,7},{7,6},{8,9},{9,8},{10,11... | collective-permute-start | bytes 7077896 | tf_op jit(solution)/shard_map/ppermute | solution.py:357
  63.5 1.7 %collective-permute-start.6 = (bf16[384,384]{1,0:T(8,128)(2,1)S(1)}, bf16[384,384]{1,0:T(8,128)(2,1)S(1)}, u32[]{:S(2)}, u32[]{:S(2)}) collective-permute-start(bf16[384,384]{1,0:T(8,128)(2,1)S(1)} %experts_second.1.hidden), channel_id=1, source_target_pairs={{0,1},{1,0},{2,3},{3,2},{4,5},{5,4},{6,7},{7,6},{8,9},{9,8},{10,11... | collective-permute-start | bytes 884744 | tf_op jit(solution)/shard_map/ppermute | solution.py:357
  65.1 11.6 %copy-start.4 = (f32[32,2]{0,1:T(2,128)S(1)}, f32[32,2]{0,1:T(2,128)}, u32[]{:S(2)}) copy-start(f32[32,2]{0,1:T(2,128)} %param.27) | copy-start | bytes 772
  65.1 42.4 %copy-start.1 = (bf16[32,6144]{1,0:T(8,128)(2,1)S(1)}, bf16[32,6144]{1,0:T(8,128)(2,1)}, u32[]{:S(2)}) copy-start(bf16[32,6144]{1,0:T(8,128)(2,1)} %param.14) | copy-start | bytes 1179652
  68.3 38.0 %all-to-all-start.1 = ((bf16[64,24,768]{2,1,0:T(8,128)(2,1)}), bf16[64,24,768]{2,1,0:T(8,128)(2,1)S(1)}, u32[]{:S(2)}, u32[]{:S(2)}) async-start(bf16[64,24,768]{2,1,0:T(8,128)(2,1)} %bitcast.12), calls=%async_computation.1 | async-start | bytes 4718592 | tf_op jit(solution)/shard_map/all_to_all | solution.py:31

commit v6 on v5

--- a/solution.py
+++ b/solution.py
@@ -400,7 +400,7 @@
         lax.ppermute(
             first[s].astype(jnp.bfloat16), "y", [(i, (i + s) % chips_y) for i in range(chips_y)]
         )
-        for s in range(1, chips_y)
+        for s in (1, 3, 2)
     ]
     gains = norm_gain.reshape(ways, share)
     first, gains, gate_weight, up_weight, down_weight = lax.optimization_barrier(

time: 108 us -> 107 us (level)
  transfers between devices with their start and end apart: 8 -> 8, of which waited for: 4 -> 5; matrix products, arithmetic and copies ran while one was open for 1% -> 1% of each run, Pallas kernels for 6% -> 6%
where the time goes in v6:
time: 107 us
  blocking collectives  39.1 us (37%)
  waiting for transfers between devices  33 us (31%)
  Pallas kernels  18 us (17%)
  starting transfers between devices  14.3 us (13%)
  matrix products  1.21 us (1%)
    all_to_all x1, blocking collectives, exchange(): lax.all_to_all(flat, EVERY, split_axis=0, concat_axis=0, axis_index_group...  39.1 us
    all_to_all x1, waiting for transfers between devices, exchange(): lax.all_to_all(flat, EVERY, split_axis=0, concat_axis=0, axis_index_group...  29.3 us
    all_to_all x1, starting transfers between devices, exchange(): lax.all_to_all(flat, EVERY, split_axis=0, concat_axis=0, axis_index_group...  8.54 us
    pallas_call x1, Pallas kernels, attend(): pl.pallas_call(attend_kernel, in_specs=[scalars] + [outside] * 7, out_spe...  6.02 us
    ppermute x3, starting transfers between devices, layer_block(): lax.ppermute(first[s].astype(jnp.bfloat16), 'y', [(i, (i + s) % chips_y)...  5.38 us
    pallas_call x1, Pallas kernels, experts_first(): pl.pallas_call(first_kernel, in_specs=[pl.BlockSpec(memory_space=pltpu.SM...  3.2 us
    pallas_call x1, Pallas kernels, experts_out(): pl.pallas_call(out_kernel, in_specs=[pl.BlockSpec(memory_space=pltpu.SMEM...  3.18 us
    ppermute x4, waiting for transfers between devices, swap(): return lax.ppermute(value, 'core', [(0, 1), (1, 0)])  3.08 us
  transfers between devices with their start and end apart: 8, of which 5 were waited for; matrix products, arithmetic and copies ran while one was open for 1% of the time, Pallas kernels for 6%

profile of v6, /device:TPU:0, one launch (start us, length us, event | category | flops | bytes accessed | tf_op | source)
XLA Modules:
  0.0 107.0 jit_solution(7995528367911084430)
XLA Ops:
  0.0 0.0 copy-start
  0.0 0.1 pad_add_fusion.place
  0.1 6.0 %attend.1 = (bf16[4,32,768]{2,1,0:T(8,128)(2,1)S(1)}, bf16[32,768]{1,0:T(8,128)(2,1)S(1)}, bf16[4,768,768]{2,1,0:T(8,128)(2,1)S(1)}) custom-call(s32[2]{0:T(128)S(1)} %pad_add_fusion.place, s32[1,32]{1,0:T(1,128)} %bitcast.42, bf16[32,768]{1,0:T(8,128)(2,1)} %queries, bf16[32,128]{1,0:T(8,128)(2,1)} %new_keys.1, bf16[32,128]{1,0:T(8,128)(2,1)} %new_values.1, ...), custom_call_target="tpu_custom_call" | custom-call | flops 150994944 | bytes 15728640 | tf_op jit(solution)/shard_map/attend/pallas_call | solution.py:129
  6.1 0.0 copy-start.3
  6.1 0.0 copy-start.2
  6.1 0.1 collective-permute-start
  6.2 0.9 project.1
  7.1 0.0 copy-done
  7.1 0.1 constant_dynamic-slice_fusion
  7.2 0.0 copy-done.3
  7.2 0.1 compare_reduce_fusion
  7.3 0.3 collective-permute-done
  7.7 1.7 %collective-permute-start.1 = (bf16[32,768]{1,0:T(8,128)(2,1)S(1)}, bf16[32,768]{1,0:T(8,128)(2,1)S(1)}, u32[]{:S(2)}, u32[]{:S(2)}) collective-permute-start(bf16[32,768]{1,0:T(8,128)(2,1)S(1)} %get-tuple-element.51), channel_id=1, source_target_pairs={{0,2},{2,4},{4,6},{6,0},{1,3},{3,5},{5,7},{7,1},{8,10},{10,12},{12... | collective-permute-start | bytes 147464 | tf_op jit(solution)/shard_map/ppermute | solution.py:400
  9.5 1.6 %collective-permute-start.2 = (bf16[32,768]{1,0:T(8,128)(2,1)S(1)}, bf16[32,768]{1,0:T(8,128)(2,1)S(1)}, u32[]{:S(2)}, u32[]{:S(2)}) collective-permute-start(bf16[32,768]{1,0:T(8,128)(2,1)S(1)} %get-tuple-element.50), channel_id=1, source_target_pairs={{0,6},{2,0},{4,2},{6,4},{1,7},{3,1},{5,3},{7,5},{8,14},{10,8},{12,... | collective-permute-start | bytes 147464 | tf_op jit(solution)/shard_map/ppermute | solution.py:400
  11.0 2.1 %collective-permute-start.3 = (bf16[32,768]{1,0:T(8,128)(2,1)S(1)}, bf16[32,768]{1,0:T(8,128)(2,1)S(1)}, u32[]{:S(2)}, u32[]{:S(2)}) collective-permute-start(bf16[32,768]{1,0:T(8,128)(2,1)S(1)} %get-tuple-element.49), channel_id=1, source_target_pairs={{0,4},{2,6},{4,0},{6,2},{1,5},{3,7},{5,1},{7,3},{8,12},{10,14},{12... | collective-permute-start | bytes 147464 | tf_op jit(solution)/shard_map/ppermute | solution.py:400
  13.1 0.1 convolution_convert_fusion.1
  13.2 0.0 copy-done.2
  13.2 0.1 dynamic_slice.7
  13.3 0.1 eq.45
  13.4 0.1 fusion.6
  13.5 0.1 collective-permute-start.5
  13.6 2.4 %load_weights.1.weight = bf16[4,768,768]{2,1,0:T(8,128)(2,1)S(1)} custom-call(s32[1]{0:T(128)} %bitcast.core, bf16[6144,384]{1,0:T(8,128)(2,1)} %gate.1, bf16[6144,384]{1,0:T(8,128)(2,1)} %up.1), custom_call_target="tpu_custom_call" | custom-call | bytes 9437184 | tf_op jit(solution)/shard_map/load_weights/pallas_call | solution.py:199
  16.0 0.0 collective-permute-done.1
  16.0 0.0 collective-permute-done.2
  16.0 0.6 collective-permute-done.3
  16.6 0.2 convolution_convert_fusion
  16.8 0.2 broadcast_in_dim.46
  17.0 39.1 %all_to_all.10 = bf16[64,24,768]{2,1,0:T(8,128)(2,1)S(1)} all-to-all(bf16[64,24,768]{2,1,0:T(8,128)(2,1)S(1)} %bitcast.40), channel_id=1, replica_groups={{0,8,16,24,32,40,48,56,64,72,80,88,96,104,112,120,2,10,18,26,34,42,50,5..., dimensions={0} | all-to-all | bytes 4718592 | tf_op jit(solution)/shard_map/all_to_all | solution.py:31
  56.1 0.0 collective-permute-start.4
  56.1 0.0 collective-permute-done.5.down_other
  56.1 3.2 %experts_first.1 = (f32[384,768]{1,0:T(8,128)S(1)}, f32[384,128]{1,0:T(8,128)S(1)}, bf16[4,768,768]{2,1,0:T(8,128)(2,1)S(1)}, bf16[4,768,768]{2,1,0:T(8,128)(2,1)S(1)}) custom-call(s32[1]{0:T(128)} %bitcast.core, bf16[4,4,4,24,768]{4,3,2,1,0:T(8,128)(2,1)S(1)} %bitcast.38, f32[8,768]{1,0:T(8,128)S(1)} %reshape.38.gain, ...), custom_call_target="tpu_custom_call" | custom-call | flops 1811939328 | bytes 12582912 | tf_op jit(solution)/shard_map/experts_first/pallas_call | solution.py:299
  59.3 1.3 %collective-permute-done.4.other = bf16[4,4,4,24,768]{4,3,2,1,0:T(8,128)(2,1)S(1)} collective-permute-done((bf16[4,4,4,24,768]{4,3,2,1,0:T(8,128)(2,1)S(1)}, bf16[4,4,4,24,768]{4,3,2,1,0:T(8,128)(2,1)S(1)}, u32[]{:S(2)}, u32[]{:S(2)}) %collective-permute-start.4) | collective-permute-done | bytes 2359328 | tf_op jit(solution)/shard_map/ppermute | solution.py:357
  60.7 2.4 %experts_second.1.hidden = bf16[384,384]{1,0:T(8,128)(2,1)S(1)} custom-call(s32[1]{0:T(128)} %bitcast.core, bf16[4,4,4,24,768]{4,3,2,1,0:T(8,128)(2,1)S(1)} %collective-permute-done.4.other, f32[8,768]{1,0:T(8,128)S(1)} %reshape.38.gain, bf16[4,768,768]{2,1,0:T(8,128)(2,1)S(1)} %get-tuple-element.43.weight, f32[384,768]{1,0:T(8,128)S(1)} %get-tuple-element.44.total_ref, ...), custom_call_target="tpu_custom_call" | custom-call | flops 1811939328 | bytes 12582912 | tf_op jit(solution)/shard_map/experts_second/pallas_call | solution.py:322
  63.0 0.2 collective-permute-start.6
  63.2 1.4 %collective-permute-done.6.hidden_other = bf16[384,384]{1,0:T(8,128)(2,1)S(1)} collective-permute-done((bf16[384,384]{1,0:T(8,128)(2,1)S(1)}, bf16[384,384]{1,0:T(8,128)(2,1)S(1)}, u32[]{:S(2)}, u32[]{:S(2)}) %collective-permute-start.6) | collective-permute-done | bytes 294944 | tf_op jit(solution)/shard_map/ppermute | solution.py:357
  64.7 0.0 copy-start.4
  64.7 0.0 copy-start.1
  64.7 3.2 %experts_out.1 = bf16[4,4,4,24,768]{4,3,2,1,0:T(8,128)(2,1)} custom-call(s32[1]{0:T(128)} %bitcast.core, bf16[384,384]{1,0:T(8,128)(2,1)S(1)} %experts_second.1.hidden, bf16[384,384]{1,0:T(8,128)(2,1)S(1)} %collective-permute-done.6.hidden_other, bf16[4,768,768]{2,1,0:T(8,128)(2,1)S(1)} %get-tuple-element.46.weight), custom_call_target="tpu_custom_call" | custom-call | flops 1811939328 | bytes 8388608 | tf_op jit(solution)/shard_map/experts_out/pallas_call | solution.py:339
  67.9 8.5 %all-to-all-start.1 = ((bf16[64,24,768]{2,1,0:T(8,128)(2,1)}), bf16[64,24,768]{2,1,0:T(8,128)(2,1)S(1)}, u32[]{:S(2)}, u32[]{:S(2)}) async-start(bf16[64,24,768]{2,1,0:T(8,128)(2,1)} %bitcast.12), calls=%async_computation.1 | async-start | bytes 4718592 | tf_op jit(solution)/shard_map/all_to_all | solution.py:31
  76.4 0.0 copy-done.4
  76.4 0.1 fusion.11
  76.5 29.3 %all-to-all-done.1 = bf16[64,24,768]{2,1,0:T(8,128)(2,1)S(1)} async-done(((bf16[64,24,768]{2,1,0:T(8,128)(2,1)}), bf16[64,24,768]{2,1,0:T(8,128)(2,1)S(1)}, u32[]{:S(2)}, u32[]{:S(2)}) %all-to-all-start.1) | async-done | bytes 2359328 | tf_op jit(solution)/shard_map/all_to_all | solution.py:31
  105.8 0.3 convert_reduce_fusion
  106.1 0.9 fusion
  107.0 0.0 copy-done.1
  (5 shorter events, 0.1 us)
Async XLA Ops:
  0.0 7.1 %copy-start = (bf16[32,6144]{1,0:T(8,128)(2,1)S(1)}, bf16[32,6144]{1,0:T(8,128)(2,1)}, u32[]{:S(2)}) copy-start(bf16[32,6144]{1,0:T(8,128)(2,1)} %param.14) | copy-start | bytes 1179652
  6.1 1.1 %copy-start.3 = (s32[32,2]{0,1:T(2,128)S(1)}, s32[32,2]{0,1:T(2,128)}, u32[]{:S(2)}) copy-start(s32[32,2]{0,1:T(2,128)} %param.26) | copy-start | bytes 772
  6.1 7.1 %copy-start.2 = (f32[6144]{0:T(1024)S(1)}, f32[6144]{0:T(1024)}, u32[]{:S(2)}) copy-start(f32[6144]{0:T(1024)} %param.22) | copy-start | bytes 73732
  6.1 1.5 %collective-permute-start = (bf16[4,32,768]{2,1,0:T(8,128)(2,1)S(1)}, bf16[4,32,768]{2,1,0:T(8,128)(2,1)S(1)}, u32[]{:S(2)}, u32[]{:S(2)}) collective-permute-start(bf16[4,32,768]{2,1,0:T(8,128)(2,1)S(1)} %get-tuple-element.32), channel_id=1, source_target_pairs={{0,1},{1,0},{2,3},{3,2},{4,5},{5,4},{6,7},{7,6},{8,9},{9,8},{10,11... | collective-permute-start | bytes 589832 | tf_op jit(solution)/shard_map/ppermute | solution.py:357
  7.7 8.3 %collective-permute-start.1 = (bf16[32,768]{1,0:T(8,128)(2,1)S(1)}, bf16[32,768]{1,0:T(8,128)(2,1)S(1)}, u32[]{:S(2)}, u32[]{:S(2)}) collective-permute-start(bf16[32,768]{1,0:T(8,128)(2,1)S(1)} %get-tuple-element.51), channel_id=1, source_target_pairs={{0,2},{2,4},{4,6},{6,0},{1,3},{3,5},{5,7},{7,1},{8,10},{10,12},{12... | collective-permute-start | bytes 147464 | tf_op jit(solution)/shard_map/ppermute | solution.py:400
  9.5 6.6 %collective-permute-start.2 = (bf16[32,768]{1,0:T(8,128)(2,1)S(1)}, bf16[32,768]{1,0:T(8,128)(2,1)S(1)}, u32[]{:S(2)}, u32[]{:S(2)}) collective-permute-start(bf16[32,768]{1,0:T(8,128)(2,1)S(1)} %get-tuple-element.50), channel_id=1, source_target_pairs={{0,6},{2,0},{4,2},{6,4},{1,7},{3,1},{5,3},{7,5},{8,14},{10,8},{12,... | collective-permute-start | bytes 147464 | tf_op jit(solution)/shard_map/ppermute | solution.py:400
  11.0 5.6 %collective-permute-start.3 = (bf16[32,768]{1,0:T(8,128)(2,1)S(1)}, bf16[32,768]{1,0:T(8,128)(2,1)S(1)}, u32[]{:S(2)}, u32[]{:S(2)}) collective-permute-start(bf16[32,768]{1,0:T(8,128)(2,1)S(1)} %get-tuple-element.49), channel_id=1, source_target_pairs={{0,4},{2,6},{4,0},{6,2},{1,5},{3,7},{5,1},{7,3},{8,12},{10,14},{12... | collective-permute-start | bytes 147464 | tf_op jit(solution)/shard_map/ppermute | solution.py:400
  13.5 42.6 %collective-permute-start.5 = (bf16[384,6144]{1,0:T(8,128)(2,1)}, bf16[384,6144]{1,0:T(8,128)(2,1)S(1)}, u32[]{:S(2)}, u32[]{:S(2)}) collective-permute-start(bf16[384,6144]{1,0:T(8,128)(2,1)} %down), channel_id=1, source_target_pairs={{0,1},{1,0},{2,3},{3,2},{4,5},{5,4},{6,7},{7,6},{8,9},{9,8},{10,11... | collective-permute-start | bytes 14155784 | tf_op jit(solution)/shard_map/ppermute | solution.py:357
  56.1 4.5 %collective-permute-start.4 = (bf16[4,4,4,24,768]{4,3,2,1,0:T(8,128)(2,1)S(1)}, bf16[4,4,4,24,768]{4,3,2,1,0:T(8,128)(2,1)S(1)}, u32[]{:S(2)}, u32[]{:S(2)}) collective-permute-start(bf16[4,4,4,24,768]{4,3,2,1,0:T(8,128)(2,1)S(1)} %bitcast.37), channel_id=1, source_target_pairs={{0,1},{1,0},{2,3},{3,2},{4,5},{5,4},{6,7},{7,6},{8,9},{9,8},{10,11... | collective-permute-start | bytes 7077896 | tf_op jit(solution)/shard_map/ppermute | solution.py:357
  63.0 1.7 %collective-permute-start.6 = (bf16[384,384]{1,0:T(8,128)(2,1)S(1)}, bf16[384,384]{1,0:T(8,128)(2,1)S(1)}, u32[]{:S(2)}, u32[]{:S(2)}) collective-permute-start(bf16[384,384]{1,0:T(8,128)(2,1)S(1)} %experts_second.1.hidden), channel_id=1, source_target_pairs={{0,1},{1,0},{2,3},{3,2},{4,5},{5,4},{6,7},{7,6},{8,9},{9,8},{10,11... | collective-permute-start | bytes 884744 | tf_op jit(solution)/shard_map/ppermute | solution.py:357
  64.7 11.7 %copy-start.4 = (f32[32,2]{0,1:T(2,128)S(1)}, f32[32,2]{0,1:T(2,128)}, u32[]{:S(2)}) copy-start(f32[32,2]{0,1:T(2,128)} %param.27) | copy-start | bytes 772
  64.7 42.3 %copy-start.1 = (bf16[32,6144]{1,0:T(8,128)(2,1)S(1)}, bf16[32,6144]{1,0:T(8,128)(2,1)}, u32[]{:S(2)}) copy-start(bf16[32,6144]{1,0:T(8,128)(2,1)} %param.14) | copy-start | bytes 1179652
  67.9 37.9 %all-to-all-start.1 = ((bf16[64,24,768]{2,1,0:T(8,128)(2,1)}), bf16[64,24,768]{2,1,0:T(8,128)(2,1)S(1)}, u32[]{:S(2)}, u32[]{:S(2)}) async-start(bf16[64,24,768]{2,1,0:T(8,128)(2,1)} %bitcast.12), calls=%async_computation.1 | async-start | bytes 4718592 | tf_op jit(solution)/shard_map/all_to_all | solution.py:31
